TPU v7x, 32 devices: a whole 2x2x4 slice. The times are simulated.
32 devices in a mesh: ctx: 8 (over z, y), tp: 4 (over x, core).
Axes of the slice: x: 2, y: 2, z: 4, core: 2. Of those that a mesh axis runs over, the one named last changes fastest.
Arguments:
- queries: bfloat16 [1024, 32, 128], P('ctx', 'tp'), may hold values from -25 to 25
- key_vectors: bfloat16 [1024, 4, 128], P('ctx', 'tp'), may hold values from -6 to 6
- value_vectors: bfloat16 [1024, 4, 128], P('ctx', 'tp'), may hold values from -6 to 6
- attention_out: bfloat16 [1024, 32, 128], P('ctx', 'tp'), may hold values from -6 to 6
- grad_attention: bfloat16 [1024, 32, 128], P('ctx', 'tp'), may hold values from -6 to 6
- mix_input: bfloat16 [1024, 8192], P('ctx', 'tp'), may hold values from -0.125 to 0.125
- grad_mix: bfloat16 [1024, 8192], P('ctx', 'tp'), may hold values from -6 to 6
- input_map: float32 [1024, 16], P('ctx'), may hold values from -0.625 to 0.625
- output_map: float32 [1024, 16], P('ctx'), may hold values from -0.625 to 0.625
- decay_log: float32 [1024, 128], P('ctx', 'tp'), may hold values from -0.6 to 0
Outputs:
- grad_queries: bfloat16 [1024, 32, 128], P('ctx', 'tp')
- grad_keys: bfloat16 [1024, 4, 128], P('ctx', 'tp')
- grad_values: bfloat16 [1024, 4, 128], P('ctx', 'tp')
- grad_input: bfloat16 [1024, 8192], P('ctx', 'tp')
- grad_input_map: float32 [1024, 16], P('ctx')
- grad_output_map: float32 [1024, 16], P('ctx')
- grad_decay: float32 [1024, 128], P('ctx', 'tp')
All inputs are finite; a program needn't handle non-finite values.
Results may differ from a plain program's by a relative error of at most 0.0052.
Values may be sent and summed in bfloat16 or wider, within the bound.
A program may use at most 128 MiB of HBM per device.

v0:
```python
import math

import jax
import jax.numpy as jnp
from jax import lax
from jax.sharding import PartitionSpec as P


def carried_in(x, axis, combine, identity, reverse):
    length, here = (lax.axis_size(axis), lax.axis_index(axis))
    everything = jax.tree.map(lambda part: lax.all_gather(part, axis), x)
    start = jax.tree.map(
        lambda part, zero: jnp.broadcast_to(jnp.asarray(zero, part.dtype), part.shape), x, identity
    )

    def turn(k, before):
        at = length - 1 - k if reverse else k
        reached = at > here if reverse else at < here
        new = combine(before, jax.tree.map(lambda part: part[at], everything))
        return jax.tree.map(lambda a, b: jnp.where(reached, a, b), new, before)

    return lax.fori_loop(0, length, turn, start)


def blend_states(earlier, later):
    decay_early, state_early = earlier
    decay_later, state_later = later
    return (decay_early * decay_later, decay_later[..., None, None] * state_early + state_later)


def attention_grads(queries, key_vectors, value_vectors, attention_out, grad_attention):
    local_rows, local_heads, head_width = queries.shape
    local_groups = key_vectors.shape[1]
    repeats = local_heads // local_groups
    score_scale = 1.0 / math.sqrt(head_width)
    whole_keys, whole_values = (
        lax.all_gather(key_vectors, "ctx", axis=0, tiled=True),
        lax.all_gather(value_vectors, "ctx", axis=0, tiled=True),
    )
    all_tokens = whole_keys.shape[0]
    key_block = math.gcd(all_tokens, 1024)
    here = lax.axis_index("ctx")

    def scores_of(entry, first_row, length):
        query_grp, query_pos = (entry[0], entry[3])
        key_part = lax.dynamic_slice_in_dim(whole_keys, first_row, length, 0)
        scores = (
            jnp.einsum("tgrd,kgd->gtrk", query_grp, key_part, preferred_element_type=jnp.float32)
            * score_scale
        )
        key_pos = first_row + jnp.arange(length)
        allowed = key_pos[None, :] <= query_pos[:, None]
        return (jnp.where(allowed[None, :, None, :], scores, -jnp.inf), key_part)

    first_pos = here * local_rows
    row_count = queries.shape[0]
    query_grp = queries.reshape(row_count, local_groups, repeats, head_width)
    grad_grp = grad_attention.reshape(row_count, local_groups, repeats, head_width)
    out_dots = jnp.sum(
        grad_attention.astype(jnp.float32) * attention_out.astype(jnp.float32), axis=-1
    )
    out_dots = out_dots.reshape(row_count, local_groups, repeats).transpose(1, 0, 2)
    query_pos = first_pos + jnp.arange(row_count)
    last_query = first_pos + row_count - 1
    live_blocks = last_query // key_block + 1
    partial_entry = (query_grp, grad_grp, out_dots, query_pos)

    def stats_step(block_index, carry):
        run_max, run_total = carry
        scores, unused_keys = scores_of(partial_entry, block_index * key_block, key_block)
        new_max = jnp.maximum(run_max, jnp.max(scores, axis=-1))
        run_total = run_total * jnp.exp(run_max - new_max) + jnp.sum(
            jnp.exp(scores - new_max[..., None]), axis=-1
        )
        return (new_max, run_total)

    start_max = jnp.full((local_groups, row_count, repeats), -jnp.inf, jnp.float32)
    start_total = jnp.zeros((local_groups, row_count, repeats), jnp.float32)
    run_max, run_total = lax.fori_loop(0, live_blocks, stats_step, (start_max, start_total))
    log_total = run_max + jnp.log(run_total)
    entries = (query_grp, grad_grp, out_dots, query_pos, last_query, live_blocks, log_total)

    def block_terms(entry, first_row, length):
        query_grp, grad_grp, out_dots, log_total = (entry[0], entry[1], entry[2], entry[6])
        scores, key_part = scores_of(entry, first_row, length)
        value_part = lax.dynamic_slice_in_dim(whole_values, first_row, length, 0)
        probs = jnp.exp(scores - log_total[..., None])
        grad_probs = jnp.einsum(
            "tgrd,kgd->gtrk", grad_grp, value_part, preferred_element_type=jnp.float32
        )
        grad_scores = (probs * (grad_probs - out_dots[..., None]) * score_scale).astype(
            jnp.bfloat16
        )
        query_add = None
        key_term = None
        query_add = jnp.einsum(
            "gtrk,kgd->tgrd", grad_scores, key_part, preferred_element_type=jnp.float32
        )
        probs_low = probs.astype(jnp.bfloat16)
        value_term = jnp.einsum(
            "gtrk,tgrd->kgd", probs_low, grad_grp, preferred_element_type=jnp.float32
        )
        keys_term = jnp.einsum(
            "gtrk,tgrd->kgd", grad_scores, query_grp, preferred_element_type=jnp.float32
        )
        key_term = jnp.stack([keys_term, value_term], axis=1)
        return (query_add, key_term)

    buffer = jnp.zeros((all_tokens, 2, local_groups, head_width), jnp.float32)
    entry = entries

    def joint_step(block_index, carry, entry=entry):
        query_acc, acc = carry
        first_row = block_index * key_block
        query_add, key_term = block_terms(entry, first_row, key_block)
        current = lax.dynamic_slice_in_dim(acc, first_row, key_block, 0)
        return (
            query_acc + query_add,
            lax.dynamic_update_slice_in_dim(acc, current + key_term, first_row, 0),
        )

    query_start = jnp.zeros(entry[0].shape, jnp.float32)
    query_acc, buffer = lax.fori_loop(0, entry[5], joint_step, (query_start, buffer))
    key_rows = lax.psum_scatter(buffer, "ctx", scatter_dimension=0, tiled=True)
    grad_queries = query_acc.reshape(local_rows, local_heads, head_width).astype(jnp.bfloat16)
    return (grad_queries, key_rows[:, 0].astype(jnp.bfloat16), key_rows[:, 1].astype(jnp.bfloat16))


def mixer_grads(mix_input, grad_mix, input_map, output_map, decay_log):
    local_rows, channels = mix_input.shape
    local_heads = decay_log.shape[1]
    head_width = channels // local_heads
    state_size = input_map.shape[1]
    span_len = math.gcd(local_rows, 128)
    span_count = local_rows // span_len
    highest = lax.Precision.HIGHEST
    inputs_f = mix_input.astype(jnp.float32).reshape(span_count, span_len, local_heads, head_width)
    grads_f = grad_mix.astype(jnp.float32).reshape(span_count, span_len, local_heads, head_width)
    in_maps = input_map.reshape(span_count, span_len, state_size)
    out_maps = output_map.reshape(span_count, span_len, state_size)
    cum_log = jnp.cumsum(decay_log.reshape(span_count, span_len, local_heads), axis=1)
    total_log = cum_log[:, -1]
    to_end = jnp.exp(total_log[:, None, :] - cum_log)
    from_start = jnp.exp(cum_log)
    span_decay = jnp.exp(total_log)
    ends = jnp.einsum("cshp,csn->chpn", inputs_f * to_end[..., None], in_maps, precision=highest)
    pulls = jnp.einsum(
        "cshp,csn->chpn", grads_f * from_start[..., None], out_maps, precision=highest
    )
    fwd_decay, fwd_state = lax.associative_scan(blend_states, (span_decay, ends), axis=0)
    bwd_decay, bwd_state = lax.associative_scan(
        blend_states, (span_decay[::-1], pulls[::-1]), axis=0
    )
    bwd_decay = bwd_decay[::-1]
    bwd_state = bwd_state[::-1]
    identity = (
        jnp.ones((local_heads,), jnp.float32),
        jnp.zeros((local_heads, head_width, state_size), jnp.float32),
    )
    unused_a, state_in = carried_in(
        (fwd_decay[-1], fwd_state[-1]), "ctx", blend_states, identity, False
    )
    unused_b, pull_out = carried_in(
        (bwd_decay[0], bwd_state[0]), "ctx", blend_states, identity, True
    )
    ones_row = jnp.ones((1, local_heads), jnp.float32)
    zero_row = jnp.zeros((1, local_heads, head_width, state_size), jnp.float32)
    prev_decay = jnp.concatenate([ones_row, fwd_decay[:-1]], axis=0)
    prev_state = jnp.concatenate([zero_row, fwd_state[:-1]], axis=0)
    start_states = prev_decay[..., None, None] * state_in[None] + prev_state
    next_decay = jnp.concatenate([bwd_decay[1:], ones_row], axis=0)
    next_pull = jnp.concatenate([bwd_state[1:], zero_row], axis=0)
    end_pulls = next_decay[..., None, None] * pull_out[None] + next_pull
    token_positions = jnp.arange(span_len)
    lower = token_positions[:, None] >= token_positions[None, :]
    cum_heads = cum_log.transpose(0, 2, 1)
    log_gap = cum_heads[:, :, :, None] - cum_heads[:, :, None, :]
    decay_mat = jnp.exp(jnp.where(lower[None, None], log_gap, -jnp.inf))
    map_dots = jnp.einsum("ctn,csn->cts", out_maps, in_maps, precision=highest)
    weights = decay_mat * map_dots[:, None]
    grad_in_f = jnp.einsum("chts,cthp->cshp", weights, grads_f, precision=highest)
    grad_in_f = grad_in_f + to_end[..., None] * jnp.einsum(
        "chpn,csn->cshp", end_pulls, in_maps, precision=highest
    )
    pair_dots = jnp.einsum("cthp,cshp->chts", grads_f, inputs_f, precision=highest)
    kernel = decay_mat * pair_dots
    kernel_sum = jnp.sum(kernel, axis=1)
    in_map_part = jnp.einsum("cts,ctn->csn", kernel_sum, out_maps, precision=highest)
    in_map_part = in_map_part + jnp.einsum(
        "csh,cshp,chpn->csn", to_end, inputs_f, end_pulls, precision=highest
    )
    out_map_part = jnp.einsum("cts,csn->ctn", kernel_sum, in_maps, precision=highest)
    out_map_part = out_map_part + jnp.einsum(
        "cth,cthp,chpn->ctn", from_start, grads_f, start_states, precision=highest
    )
    grad_in_map, grad_out_map = lax.psum(
        (in_map_part.reshape(local_rows, state_size), out_map_part.reshape(local_rows, state_size)),
        "tp",
    )
    mixed = kernel * map_dots[:, None]
    row_part = jnp.sum(mixed, axis=-1).transpose(0, 2, 1)
    col_part = jnp.sum(mixed, axis=-2).transpose(0, 2, 1)
    start_part = from_start * jnp.einsum(
        "cthp,chpn,ctn->cth", grads_f, start_states, out_maps, precision=highest
    )
    end_part = to_end * jnp.einsum(
        "cshp,chpn,csn->csh", inputs_f, end_pulls, in_maps, precision=highest
    )
    end_total = jnp.sum(end_part, axis=1) + span_decay * jnp.sum(
        end_pulls * start_states, axis=(2, 3)
    )
    per_log = row_part - col_part + start_part - end_part
    suffix = jnp.cumsum(per_log[:, ::-1], axis=1)[:, ::-1]
    grad_decay = (suffix + end_total[:, None, :]).reshape(local_rows, local_heads)
    grad_input = grad_in_f.reshape(local_rows, channels).astype(jnp.bfloat16)
    return (grad_input, grad_in_map, grad_out_map, grad_decay)


def local(
    queries,
    key_vectors,
    value_vectors,
    attention_out,
    grad_attention,
    mix_input,
    grad_mix,
    input_map,
    output_map,
    decay_log,
):
    grad_queries, grad_keys, grad_values = attention_grads(
        queries, key_vectors, value_vectors, attention_out, grad_attention
    )
    grad_input, grad_in_map, grad_out_map, grad_decay = mixer_grads(
        mix_input, grad_mix, input_map, output_map, decay_log
    )
    return (grad_queries, grad_keys, grad_values, grad_input, grad_in_map, grad_out_map, grad_decay)


def solution(mesh):
    in_specs = (
        P("ctx", "tp", None),
        P("ctx", "tp", None),
        P("ctx", "tp", None),
        P("ctx", "tp", None),
        P("ctx", "tp", None),
        P("ctx", "tp"),
        P("ctx", "tp"),
        P("ctx", None),
        P("ctx", None),
        P("ctx", "tp"),
    )
    out_specs = (
        P("ctx", "tp", None),
        P("ctx", "tp", None),
        P("ctx", "tp", None),
        P("ctx", "tp"),
        P("ctx", None),
        P("ctx", None),
        P("ctx", "tp"),
    )
    return jax.shard_map(local, mesh=mesh, in_specs=in_specs, out_specs=out_specs, check_vma=False)
```

profile of v0, /device:TPU:25, one launch (start us, length us, event | category | flops | bytes accessed | tf_op | source)
XLA Modules:
  0.0 232.0 jit_solution(16598551252442627872)
XLA Ops:
  8.1 1.3 copy.80
  9.8 4.0 %fusion.53 = f32[32,64,16]{1,2,0:T(8,128)} fusion(f32[128,32,64]{0,2,1:T(8,128)S(1)} %bitcast.237, f32[128,16]{0,1:T(8,128)} %param.26), kind=kOutput, calls=%fused_computation.85 | convolution fusion | flops 50331648 | bytes 1187840 | tf_op jit(solution)/shard_map/cshp,csn->chpn/dot_general | solution.py:147
  13.8 22.7 %all_gather.16 = bf16[1024,1,128]{2,0,1:T(8,128)(2,1)S(1)} all-gather(bf16[128,1,128]{2,0,1:T(8,128)(2,1)S(1)} %copy-done.9), channel_id=1, replica_groups=mesh['ctx'=8,'tp'=4] {'ctx'}, dimensions={0}, use_global_device_ids=true | all-gather | bytes 294912 | tf_op jit(solution)/shard_map/all_gather | solution.py:37
  37.3 2.2 while.56
  38.4 1.1 exponential_reduce_fusion.2
  39.6 25.6 %all_gather.17 = bf16[1024,1,128]{2,0,1:T(8,128)(2,1)S(1)} all-gather(bf16[128,1,128]{2,0,1:T(8,128)(2,1)S(1)} %copy-done.10), channel_id=1, replica_groups=mesh['ctx'=8,'tp'=4] {'ctx'}, dimensions={0}, use_global_device_ids=true | all-gather | bytes 294912 | tf_op jit(solution)/shard_map/all_gather | solution.py:38
  65.6 9.7 %while.57 = (s32[]{:T(128)}, f32[128,1,8,128]{3,0,2,1:T(8,128)S(1)}, f32[1024,2,1,128]{3,0,2,1:T(8,128)S(1)}, s32[]{:T(128)}, bf16[128,1,8,128]{3,0,2,1:T(8,128)...) while((s32[]{:T(128)}, ...), condition=%wide.region_6.7_spmd.clone, body=%wide.region_5.6_spmd.clone.sunk | while | flops 1354499200 | bytes 44192976 | solution.py:123
  65.6 2.6 %fusion.105 = f32[128,8,1024]{2,0,1:T(8,128)} fusion(bf16[1024,1,128]{2,0,1:T(8,128)(2,1)S(1)} %get-tuple-element.778, bf16[128,1,8,128]{3,0,2,1:T(8,128)(2,1)S(1)} %get-tuple-element.777), kind=kOutput, calls=%fused_computation.27.clone.1 | convolution fusion | flops 268435456 | bytes 4718592 | tf_op jit(solution)/shard_map/while/body/tgrd,kgd->gtrk/dot_general | solution.py:48
  68.4 3.8 %multiply_convert_fusion.2 = bf16[128,8,1024]{2,0,1:T(8,128)(2,1)S(1)} fusion(f32[128,8,1024]{2,0,1:T(8,128)} %fusion.105, f32[128,8]{0,1:T(8,128)S(1)} %get-tuple-element.782, f32[128,8]{0,1:T(8,128)S(1)} %bitcast.246, pred[128,1024]{1,0:T(8,128)(4,1)S(1)} %broadcast_compare_fusion.5, bf16[1024,1,128]{2,0,1:T(8,128)(2,1)S(1)} %get-tuple-element.781, ...), kind=kOutput, calls=%fused_computation.13.clone.1 | convolution fusion | flops 275775488 | bytes 6955008 | tf_op jit(solution)/shard_map/while/body/tgrd,kgd->gtrk/dot_general | solution.py:88
  73.0 1.2 fusion.107
  76.3 14.2 %all-gather = f32[8,1,32]{2,1,0:T(1,128)S(1)} all-gather(f32[1,1,32]{2,1,0:T(1,128)S(1)} %get-tuple-element.533), channel_id=2, replica_groups=mesh['ctx'=8,'tp'=4] {'ctx'}, dimensions={0}, use_global_device_ids=true | all-gather | bytes 1152 | tf_op jit(solution)/shard_map/all_gather | solution.py:11
  90.9 9.0 %while.58 = (s32[]{:T(128)}, f32[32,64,16]{1,2,0:T(8,128)S(1)}, s32[]{:T(128)}, f32[8,32]{1,0:T(8,128)S(1)}, f32[8,32,64,16]{2,3,1,0:T(8,128)}, /*index=5*/s32[]{:T(128)}, s32[]{:T(128)}, s32[]{:T(128)}, s32[]{:T(128)}) while((s32[]{:T(128)}, f32[32,64,16]{1,2,0:T(8,128)S(1)}, s32[]{:T(128)}, f32[8,32]{1,0:T(8,128)S(1)}, ...), condition=%wide.region_10.11_spmd.clone, body=%wide.region_9.10_spmd.clone.sunk | while | flops 131080 | bytes 393775 | solution.py:22
  90.9 1.1 fusion.108
  92.0 1.1 fusion.108
  93.2 1.1 fusion.108
  98.8 1.1 fusion.108
  100.7 3.3 %fusion.50 = f32[32,64,16]{1,2,0:T(8,128)} fusion(f32[128,32,64]{0,2,1:T(8,128)S(1)} %bitcast.238, f32[128,16]{0,1:T(8,128)S(1)} %copy-done.7), kind=kOutput, calls=%fused_computation.82 | convolution fusion | flops 50331648 | bytes 1187840 | tf_op jit(solution)/shard_map/cshp,csn->chpn/dot_general | solution.py:146
  105.4 1.7 multiply_reduce_fusion
  107.2 1.8 fusion.35
  109.0 1.8 fusion.39
  112.0 40.0 %reduce-scatter.2.cloned.1.call-done = f32[128,2,1,128]{3,0,2,1:T(8,128)} async-done(((f32[1024,2,1,128]{3,0,2,1:T(8,128)}), f32[128,2,1,128]{3,0,2,1:T(8,128)}) %reduce-scatter.2.cloned.1.call-update) | async-done | bytes 131088 | tf_op jit(solution)/shard_map/reduce_scatter | solution.py:124
  153.6 50.3 %all-gather.8.cloned.1.call-done = f32[256,64,16]{1,2,0:T(8,128)} async-done(((f32[32,64,16]{1,2,0:T(8,128)}), f32[256,64,16]{1,2,0:T(8,128)}) %all-gather.8.cloned.1.call-update) | async-done | bytes 1048592 | tf_op jit(solution)/shard_map/all_gather | solution.py:11
  203.9 8.9 %while.59 = (s32[]{:T(128)}, f32[32,64,16]{1,2,0:T(8,128)S(1)}, s32[]{:T(128)}, f32[8,32]{1,0:T(8,128)S(1)}, f32[8,32,64,16]{2,3,1,0:T(8,128)}, /*index=5*/s32[]{:T(128)}, s32[]{:T(128)}) while((s32[]{:T(128)}, f32[32,64,16]{1,2,0:T(8,128)S(1)}, s32[]{:T(128)}, f32[8,32]{1,0:T(8,128)S(1)}, f32[8,32,64,16]{2,3,1,0:T(8,128)}, ...), condition=%wide.region_14.15_spmd.clone, body=%wide.region_13.14_spmd.clone.sunk | while | flops 131076 | bytes 393713 | solution.py:22
  215.1 10.4 %all-reduce = (f32[128,16]{0,1:T(8,128)}, f32[128,16]{0,1:T(8,128)}) all-reduce(f32[128,16]{0,1:T(8,128)S(1)} %convolution_add_fusion.1, f32[128,16]{0,1:T(8,128)S(1)} %convolution_add_fusion), channel_id=1, replica_groups=mesh['ctx'=8,'tp'=4] {'tp'}, use_global_device_ids=true, to_apply=%region_12.13 | all-reduce | flops 4096 | bytes 32768 | tf_op jit(solution)/shard_map/psum | solution.py:196
  (111 shorter events, 26.9 us)
Async XLA Ops:
  7.2 6.6 %copy-start.9 = (bf16[128,1,128]{2,0,1:T(8,128)(2,1)S(1)}, bf16[128,1,128]{2,0,1:T(8,128)(2,1)}, u32[]{:S(2)}) copy-start(bf16[128,1,128]{2,0,1:T(8,128)(2,1)} %param.19) | copy-start | bytes 98308
  7.2 29.4 %copy-start.2 = (bf16[128,8,128]{2,1,0:T(8,128)(2,1)S(1)}, bf16[128,8,128]{2,1,0:T(8,128)(2,1)}, u32[]{:S(2)}) copy-start(bf16[128,8,128]{2,1,0:T(8,128)(2,1)} %param.22) | copy-start | bytes 786436
  7.2 29.3 %copy-start.5 = (bf16[128,8,128]{2,1,0:T(8,128)(2,1)S(1)}, bf16[128,8,128]{2,1,0:T(8,128)(2,1)}, u32[]{:S(2)}) copy-start(bf16[128,8,128]{2,1,0:T(8,128)(2,1)} %param.18) | copy-start | bytes 786436
  7.2 83.6 %all-gather.6.cloned.1.call-start = ((), (), s32[]{:S(2)}) async-start(), calls=%async_computation.2 | async-start | bytes 2359296 | tf_op jit(solution)/shard_map/all_gather | solution.py:11
  13.7 138.3 %reduce-scatter.2.cloned.1.call-start = ((), (), s32[]{:S(2)}) async-start(), calls=%async_computation.1 | async-start | bytes 1179648 | tf_op jit(solution)/shard_map/reduce_scatter | solution.py:124
  37.3 2.2 copy-start.10
  37.3 27.8 %copy-start.4 = (bf16[128,8,128]{2,1,0:T(8,128)(2,1)S(1)}, bf16[128,8,128]{2,1,0:T(8,128)(2,1)}, u32[]{:S(2)}) copy-start(bf16[128,8,128]{2,1,0:T(8,128)(2,1)} %param.21) | copy-start | bytes 786436
  65.5 25.0 %copy-start.3 = (bf16[128,2048]{1,0:T(8,128)(2,1)S(1)}, bf16[128,2048]{1,0:T(8,128)(2,1)}, u32[]{:S(2)}) copy-start(bf16[128,2048]{1,0:T(8,128)(2,1)} %param.23) | copy-start | bytes 1572868
  68.4 4.6 %copy-start = (f32[128,8,1024]{2,0,1:T(8,128)S(1)}, f32[128,8,1024]{2,0,1:T(8,128)}, u32[]{:S(2)}) copy-start(f32[128,8,1024]{2,0,1:T(8,128)} %fusion.105) | copy-start | bytes 12582916 | tf_op jit(solution)/shard_map/while
  68.4 4.6 %copy-start.6 = (bf16[128,1,8,128]{3,0,2,1:T(8,128)(2,1)S(1)}, bf16[128,1,8,128]{3,0,2,1:T(8,128)(2,1)}, u32[]{:S(2)}) copy-start(bf16[128,1,8,128]{3,0,2,1:T(8,128)(2,1)} %get-tuple-element.780) | copy-start | bytes 786436 | tf_op jit(solution)/shard_map/while
  75.2 1.0 copy-start.1
  75.2 24.7 %copy-start.7 = (f32[128,16]{0,1:T(8,128)S(1)}, f32[128,16]{0,1:T(8,128)}, u32[]{:S(2)}) copy-start(f32[128,16]{0,1:T(8,128)} %param.25) | copy-start | bytes 24580
  76.2 127.6 %all-gather.8.cloned.1.call-start = ((), (), s32[]{:S(2)}) async-start(), calls=%async_computation.3 | async-start | bytes 2359296 | tf_op jit(solution)/shard_map/all_gather | solution.py:11
  90.8 14.3 %copy-start.8 = (f32[128,16]{0,1:T(8,128)S(1)}, f32[128,16]{0,1:T(8,128)}, u32[]{:S(2)}) copy-start(f32[128,16]{0,1:T(8,128)} %param.26) | copy-start | bytes 24580
Sparse Core Ops, SparseCore 0:
  13.9 51.3 all-gather.5
  76.4 75.6 reduce-scatter.1
  154.4 49.4 all-gather.7
where the time goes:
time: 236 us; the launch traced here: 232 us
  waiting for transfers between devices  90.4 us (38%)
  blocking collectives  72.9 us (31%)
  matrix products  24.3 us (10%)
  other arithmetic  21.2 us (9%)
  between operations  14.1 us (6%)
  local copies, waits for them, and re-layouts  8.21 us (3%)
    all_gather x2, waiting for transfers between devices, carried_in(): everything = jax.tree.map(lambda part: lax.all_gather(part, axis), x)  50.3 us
    reduce_scatter x1, waiting for transfers between devices, attention_grads(): key_rows = lax.psum_scatter(buffer, 'ctx', scatter_dimension=0, tiled=True)  40 us
    all_gather x1, blocking collectives, attention_grads(): lax.all_gather(value_vectors, 'ctx', axis=0, tiled=True)  25.6 us
    all_gather x1, blocking collectives, attention_grads(): lax.all_gather(key_vectors, 'ctx', axis=0, tiled=True)  22.7 us
    select_n x16, other arithmetic, turn(): return jax.tree.map(lambda a, b: jnp.where(reached, a, b), new, before)  17.2 us
    all_gather x1, blocking collectives, carried_in(): everything = jax.tree.map(lambda part: lax.all_gather(part, axis), x)  14.2 us
    psum x1, blocking collectives, mixer_grads(): lax.psum((in_map_part.reshape(local_rows, state_size), out_map_part.resha...  10.4 us
  transfers between devices with their start and end apart: 3, of which 2 were waited for; matrix products, arithmetic and copies ran while one was open for 15% of the time, Pallas kernels for 0%

commit v1 on v0

v1 whole, which is shorter than its diff:
```python
import functools
import math

import jax
import jax.numpy as jnp
from jax import lax
from jax.experimental import pallas as pl
from jax.experimental.pallas import tpu as pltpu
from jax.sharding import PartitionSpec as P

F32 = jnp.float32
BF16 = jnp.bfloat16
MESH = pl.DeviceIdType.MESH
LOG2E = math.log2(math.e)
MASKED = -1e30


def mm(a, b):
    return lax.dot_general(a, b, (((1,), (0,)), ((), ())), preferred_element_type=F32)


def mm_nt(a, b):
    return lax.dot_general(a, b, (((1,), (1,)), ((), ())), preferred_element_type=F32)


def mm_full(a, b):
    return lax.dot_general(
        a, b, (((1,), (0,)), ((), ())), precision=lax.Precision.HIGHEST, preferred_element_type=F32
    )


def halves(a):
    high = a.astype(BF16)
    return high, (a - high.astype(F32)).astype(BF16)


def mm_split(a, b):
    high, low = halves(a)
    return mm(high, b) + mm(low, b)


def mm_nt_split(a, b):
    high, low = halves(a)
    return mm_nt(high, b) + mm_nt(low, b)


def kernel(
    n,
    ntp,
    heads,
    q_ref,
    k_ref,
    v_ref,
    o_ref,
    go_ref,
    x_ref,
    g_ref,
    bm_ref,
    cm_ref,
    dl_ref,
    gq_ref,
    gk_ref,
    gv_ref,
    gx_ref,
    gb_ref,
    gc_ref,
    gd_ref,
    kv,
    st,
    st_out,
    tot,
    grad_out,
    grad_in,
    tp_buf,
    gs,
    xs,
    ends_pre,
    e_wide,
    f_wide,
    half_wide,
    dots_row,
    stat_max,
    stat_sum,
    gq_t,
    kv_s,
    kv_r,
    st_s,
    st_r,
    tt_s,
    tt_r,
    gr_s,
    gr_r,
    tp_s,
    tp_r,
):
    me = lax.axis_index("ctx")
    me_tp = lax.axis_index("tp")
    tokens, channels = x_ref.shape
    groups = dl_ref.shape[1]
    state = bm_ref.shape[1]
    rows, width = q_ref.shape
    chunk = 256
    score_scale = 1.0 / math.sqrt(width)

    barrier = pltpu.get_barrier_semaphore()

    def greet_ctx(d, c):
        pl.semaphore_signal(
            barrier, inc=1, device_id={"ctx": lax.rem(me + d, n)}, device_id_type=MESH
        )
        return c

    def greet_tp(d, c):
        pl.semaphore_signal(
            barrier, inc=1, device_id={"tp": lax.rem(me_tp + d, ntp)}, device_id_type=MESH
        )
        return c

    lax.fori_loop(1, n, greet_ctx, 0)
    lax.fori_loop(1, ntp, greet_tp, 0)
    kv[me, 0:tokens, :] = k_ref[...]
    kv[me, tokens : 2 * tokens, :] = v_ref[...]
    pl.semaphore_wait(barrier, n - 1 + ntp - 1)

    def kv_copy(src, dst):
        return pltpu.make_async_remote_copy(
            src_ref=kv.at[src],
            dst_ref=kv.at[src],
            send_sem=kv_s.at[dst],
            recv_sem=kv_r.at[src],
            device_id={"ctx": dst},
            device_id_type=MESH,
        )

    def state_copy(src, dst, which):
        return pltpu.make_async_remote_copy(
            src_ref=st_out.at[which],
            dst_ref=st.at[src],
            send_sem=st_s.at[dst],
            recv_sem=st_r.at[src],
            device_id={"ctx": dst},
            device_id_type=MESH,
        )

    def tot_copy(src, dst):
        return pltpu.make_async_remote_copy(
            src_ref=tot.at[src],
            dst_ref=tot.at[src],
            send_sem=tt_s.at[dst],
            recv_sem=tt_r.at[src],
            device_id={"ctx": dst},
            device_id_type=MESH,
        )

    def grad_copy(src, dst):
        return pltpu.make_async_remote_copy(
            src_ref=grad_out.at[dst],
            dst_ref=grad_in.at[src],
            send_sem=gr_s.at[dst],
            recv_sem=gr_r.at[src],
            device_id={"ctx": dst},
            device_id_type=MESH,
        )

    def tp_copy(src, dst):
        return pltpu.make_async_remote_copy(
            src_ref=tp_buf.at[src],
            dst_ref=tp_buf.at[src],
            send_sem=tp_s.at[dst],
            recv_sem=tp_r.at[src],
            device_id={"tp": dst},
            device_id_type=MESH,
        )

    def send_kv(dst, c):
        kv_copy(me, dst).start()
        return c

    lax.fori_loop(me + 1, n, send_kv, 0)

    token_row = lax.broadcasted_iota(jnp.int32, (tokens, tokens), 0)
    token_col = lax.broadcasted_iota(jnp.int32, (tokens, tokens), 1)
    lower = token_row >= token_col
    seg = (
        lax.broadcasted_iota(jnp.int32, (groups, channels), 1) // (channels // groups)
        == lax.broadcasted_iota(jnp.int32, (groups, channels), 0)
    ).astype(F32).astype(BF16)
    cum = mm_full(lower.astype(F32), dl_ref[...])
    total = cum[tokens - 1 : tokens, :]
    mid = 0.5 * total
    e_wide[...] = mm_split(jnp.exp(cum - mid), seg)
    f_wide[...] = mm_split(jnp.exp(mid - cum), seg)
    half_wide[...] = mm_split(jnp.exp(jnp.broadcast_to(mid, (state, groups))), seg)
    gs[0:tokens, :] = (e_wide[...] * g_ref[...].astype(F32)).astype(BF16)
    xs[0:tokens, :] = (f_wide[...] * x_ref[...].astype(F32)).astype(BF16)
    in_map = bm_ref[...]
    out_map = cm_ref[...]
    maps_t = jnp.concatenate(
        [in_map, out_map, jnp.zeros((tokens, 128 - 2 * state), F32)], axis=1
    ).T
    in_map_t = maps_t[0:state, :]
    out_map_t = maps_t[state : 2 * state, :]
    ends_pre[...] = mm_split(in_map_t, xs[0:tokens, :])
    st_out[0] = (half_wide[...] * ends_pre[...]).astype(BF16)
    st_out[1] = (half_wide[...] * mm_split(out_map_t, gs[0:tokens, :])).astype(BF16)
    tot[me] = jnp.broadcast_to(
        jnp.concatenate([total, jnp.zeros((1, 128 - groups), F32)], axis=1), (8, 128)
    )

    def send_states(d, c):
        dst = lax.rem(me + d, n)
        tot_copy(me, dst).start()

        @pl.when(dst > me)
        def _():
            state_copy(me, dst, 0).start()

        @pl.when(dst < me)
        def _():
            state_copy(me, dst, 1).start()

        return c

    lax.fori_loop(1, n, send_states, 0)

    key_at = lax.broadcasted_iota(jnp.int32, (tokens, chunk), 0)
    pair_at = lax.broadcasted_iota(jnp.int32, (tokens, chunk), 1)
    ones_row = jnp.ones((8, width), BF16)

    for first in range(0, rows, chunk):
        part = pl.ds(first, chunk)
        prod = go_ref[part, :].astype(F32) * o_ref[part, :].astype(F32)
        high, low = halves(prod)
        dots_row[:, part] = mm_nt(ones_row, high) + mm_nt(ones_row, low)

    def scores_of(keys, first, diagonal):
        scores = mm_nt(keys, q_ref[pl.ds(first, chunk), :]) * (score_scale * LOG2E)
        if diagonal:
            scores = jnp.where(key_at <= (pair_at + first) // heads, scores, MASKED)
        return scores

    own_keys = k_ref[...]
    for first in range(0, rows, chunk):
        part = pl.ds(first, chunk)
        scores = scores_of(own_keys, first, True)
        top = jnp.max(scores, axis=0, keepdims=True)
        stat_max[:, part] = jnp.broadcast_to(top, (8, chunk))
        stat_sum[:, part] = jnp.broadcast_to(
            jnp.sum(jnp.exp2(scores - top), axis=0, keepdims=True), (8, chunk)
        )

    def stats_step(d, c):
        src = me - d
        kv_copy(src, me).wait_recv()
        keys = kv[src, 0:tokens, :]
        for first in range(0, rows, chunk):
            part = pl.ds(first, chunk)
            scores = scores_of(keys, first, False)
            before = stat_max[0:1, part]
            top = jnp.maximum(before, jnp.max(scores, axis=0, keepdims=True))
            summed = stat_sum[0:1, part] * jnp.exp2(before - top) + jnp.sum(
                jnp.exp2(scores - top), axis=0, keepdims=True
            )
            stat_max[:, part] = jnp.broadcast_to(top, (8, chunk))
            stat_sum[:, part] = jnp.broadcast_to(summed, (8, chunk))
        return c

    lax.fori_loop(1, me + 1, stats_step, 0)
    stat_max[...] = stat_max[...] + jnp.log(stat_sum[...]) * LOG2E
    gq_t[...] = jnp.zeros_like(gq_t)

    def grads_of(keys, values, diagonal):
        keys_t = keys.astype(F32).T.astype(BF16)
        key_sum = jnp.zeros((tokens, width), F32)
        value_sum = jnp.zeros((tokens, width), F32)
        for first in range(0, rows, chunk):
            part = pl.ds(first, chunk)
            queries = q_ref[part, :]
            grads = go_ref[part, :]
            probs = jnp.exp2(scores_of(keys, first, diagonal) - stat_max[0:1, part])
            grad_probs = mm_nt(values, grads)
            grad_scores = (probs * (grad_probs - dots_row[0:1, part]) * score_scale).astype(BF16)
            value_sum = value_sum + mm(probs.astype(BF16), grads)
            key_sum = key_sum + mm(grad_scores, queries)
            gq_t[:, part] += mm(keys_t, grad_scores)
        return key_sum, value_sum

    def grads_step(src, c):
        key_sum, value_sum = grads_of(kv[src, 0:tokens, :], kv[src, tokens : 2 * tokens, :], False)
        grad_out[src, 0:tokens, :] = key_sum.astype(BF16)
        grad_out[src, tokens : 2 * tokens, :] = value_sum.astype(BF16)
        grad_copy(me, src).start()
        return c

    lax.fori_loop(0, me, grads_step, 0)
    own_key_sum, own_value_sum = grads_of(own_keys, v_ref[...], True)
    gq_ref[...] = gq_t[...].T.astype(BF16)

    def take_states(start, src_of):
        def step(d, carry):
            summed, log_sum = carry
            src = src_of(d)
            tot_copy(src, me).wait_recv()
            state_copy(src, me, 0).wait_recv()
            summed = summed + mm_split(jnp.exp(log_sum), seg) * st[src].astype(F32)
            log_sum = log_sum + jnp.broadcast_to(tot[src][0:1, 0:groups], (state, groups))
            return summed, log_sum

        zero = (jnp.zeros((state, channels), F32), jnp.zeros((state, groups), F32))
        return lax.fori_loop(1, start, step, zero)[0]

    state_in = take_states(me + 1, lambda d: me - d) * half_wide[...]
    pull_in = take_states(n - me, lambda d: me + d) * half_wide[...]
    xs[tokens : tokens + state, :] = state_in.astype(BF16)
    gs[tokens : tokens + state, :] = pull_in.astype(BF16)
    kernel_sum = jnp.where(lower, mm_nt(gs[0:tokens, :], xs[0:tokens, :]), 0.0)
    tp_buf[me_tp, 0:state, :] = mm_full(out_map_t, kernel_sum) + mm_nt(
        gs[tokens : tokens + state, :], xs[0:tokens, :]
    )
    tp_buf[me_tp, state : 2 * state, :] = mm_full(in_map_t, kernel_sum.T) + mm_nt(
        xs[tokens : tokens + state, :], gs[0:tokens, :]
    )

    def send_tp(d, c):
        tp_copy(me_tp, lax.rem(me_tp + d, ntp)).start()
        return c

    lax.fori_loop(1, ntp, send_tp, 0)

    map_dots = jnp.where(lower, mm_full(out_map, in_map_t), 0.0)
    forward = jnp.concatenate([map_dots.astype(BF16), out_map.astype(BF16)], axis=1)
    backward = jnp.concatenate([map_dots.T.astype(BF16), in_map.astype(BF16)], axis=1)
    out_pre = mm(forward, xs[...])
    in_pre = mm(backward, gs[...])
    gx_ref[...] = (f_wide[...] * in_pre).astype(BF16)
    per_token = gs[0:tokens, :].astype(F32) * out_pre - xs[0:tokens, :].astype(F32) * in_pre
    at_end = pull_in * (state_in + ends_pre[...])
    seg_token = mm_nt_split(per_token, seg)
    seg_end = mm_nt_split(at_end, seg)
    gd_ref[...] = mm_full((token_row <= token_col).astype(F32), seg_token) + jnp.sum(
        seg_end, axis=0, keepdims=True
    )

    def take_grads(src, carry):
        grad_copy(src, me).wait_recv()
        return (
            carry[0] + grad_in[src, 0:tokens, :].astype(F32),
            carry[1] + grad_in[src, tokens : 2 * tokens, :].astype(F32),
        )

    key_total, value_total = lax.fori_loop(
        me + 1, n, take_grads, (own_key_sum, own_value_sum)
    )
    gk_ref[...] = key_total.astype(BF16)
    gv_ref[...] = value_total.astype(BF16)

    def wait_tp(d, c):
        tp_copy(lax.rem(me_tp + d, ntp), me_tp).wait_recv()
        return c

    lax.fori_loop(1, ntp, wait_tp, 0)
    map_grads = tp_buf[0]
    for other in range(1, ntp):
        map_grads = map_grads + tp_buf[other]
    map_grads = jnp.concatenate([map_grads, jnp.zeros((128 - 2 * state, tokens), F32)], axis=0).T
    gb_ref[...] = map_grads[:, 0:state]
    gc_ref[...] = map_grads[:, state : 2 * state]

    def end_tp(d, c):
        tp_copy(me_tp, lax.rem(me_tp + d, ntp)).wait_send()
        return c

    def end_states(d, c):
        dst = lax.rem(me + d, n)
        tot_copy(me, dst).wait_send()
        state_copy(me, dst, 0).wait_send()
        return c

    def end_kv(dst, c):
        kv_copy(me, dst).wait_send()
        return c

    def end_grads(dst, c):
        grad_copy(me, dst).wait_send()
        return c

    lax.fori_loop(1, ntp, end_tp, 0)
    lax.fori_loop(1, n, end_states, 0)
    lax.fori_loop(me + 1, n, end_kv, 0)
    lax.fori_loop(0, me, end_grads, 0)


def local(
    n,
    ntp,
    queries,
    key_vectors,
    value_vectors,
    attention_out,
    grad_attention,
    mix_input,
    grad_mix,
    input_map,
    output_map,
    decay_log,
):
    tokens, heads, width = queries.shape
    channels = mix_input.shape[1]
    state = input_map.shape[1]
    groups = decay_log.shape[1]
    rows = tokens * heads
    flat = lambda a: a.reshape(-1, width)
    vmem = pl.BlockSpec(memory_space=pltpu.VMEM)
    dma = pltpu.SemaphoreType.DMA
    outs = pl.pallas_call(
        functools.partial(kernel, n, ntp, heads),
        out_shape=(
            jax.ShapeDtypeStruct((rows, width), BF16),
            jax.ShapeDtypeStruct((tokens, width), BF16),
            jax.ShapeDtypeStruct((tokens, width), BF16),
            jax.ShapeDtypeStruct((tokens, channels), BF16),
            jax.ShapeDtypeStruct((tokens, state), F32),
            jax.ShapeDtypeStruct((tokens, state), F32),
            jax.ShapeDtypeStruct((tokens, groups), F32),
        ),
        in_specs=[vmem] * 10,
        out_specs=(vmem,) * 7,
        scratch_shapes=[
            pltpu.VMEM((n, 2 * tokens, width), BF16),
            pltpu.VMEM((n, state, channels), BF16),
            pltpu.VMEM((2, state, channels), BF16),
            pltpu.VMEM((n, 8, 128), F32),
            pltpu.VMEM((n, 2 * tokens, width), BF16),
            pltpu.VMEM((n, 2 * tokens, width), BF16),
            pltpu.VMEM((ntp, 2 * state, tokens), F32),
            pltpu.VMEM((tokens + state, channels), BF16),
            pltpu.VMEM((tokens + state, channels), BF16),
            pltpu.VMEM((state, channels), F32),
            pltpu.VMEM((tokens, channels), F32),
            pltpu.VMEM((tokens, channels), F32),
            pltpu.VMEM((state, channels), F32),
            pltpu.VMEM((8, rows), F32),
            pltpu.VMEM((8, rows), F32),
            pltpu.VMEM((8, rows), F32),
            pltpu.VMEM((width, rows), F32),
            dma((n,)),
            dma((n,)),
            dma((n,)),
            dma((n,)),
            dma((n,)),
            dma((n,)),
            dma((n,)),
            dma((n,)),
            dma((ntp,)),
            dma((ntp,)),
        ],
        compiler_params=pltpu.CompilerParams(
            collective_id=0, has_side_effects=True, vmem_limit_bytes=48 * 1024 * 1024
        ),
        name="layer_grads",
    )(
        flat(queries),
        flat(key_vectors),
        flat(value_vectors),
        flat(attention_out),
        flat(grad_attention),
        mix_input,
        grad_mix,
        input_map,
        output_map,
        decay_log,
    )
    return (
        outs[0].reshape(queries.shape),
        outs[1].reshape(key_vectors.shape),
        outs[2].reshape(value_vectors.shape),
    ) + tuple(outs[3:])


def solution(mesh):
    seq = P("ctx", "tp", None)
    both = P("ctx", "tp")
    ctx = P("ctx", None)
    return jax.shard_map(
        functools.partial(local, mesh.shape["ctx"], mesh.shape["tp"]),
        mesh=mesh,
        in_specs=(seq, seq, seq, seq, seq, both, both, ctx, ctx, both),
        out_specs=(seq, seq, seq, both, ctx, ctx, both),
        check_vma=False,
    )
```

time: 236 us -> 46.9 us (0.20); the launches traced: 232 us -> 46.1 us
  waiting for transfers between devices: 90.4 us -> 0 us
  blocking collectives: 72.9 us -> 0 us
  Pallas kernels: 0 us -> 32.9 us
  matrix products: 24.3 us -> 0 us
  other arithmetic: 21.2 us -> 0 us
  between operations: 14.1 us -> 0.66 us
  local copies, waits for them, and re-layouts: 8.21 us -> 12.5 us
    all_gather x3 -> x0, blocking collectives: 62.5 us -> none  [the longest x1 25.6 us: attention_grads(): lax.all_gather(value_vectors, 'ctx', axis=0, tiled=True)]
    all_gather x2 -> x0, waiting for transfers between devices: 50.3 us -> none  [carried_in(): everything = jax.tree.map(lambda part: lax.all_gather(part, axis), x)]
    reduce_scatter x1 -> x0, waiting for transfers between devices: 40 us -> none  [attention_grads(): key_rows = lax.psum_scatter(buffer, 'ctx', scatter_dimension=0, tiled=True)]
    pallas_call x0 -> x1, Pallas kernels: none -> 32.9 us  [local(): pl.pallas_call(functools.partial(kernel, n, ntp, heads), out_shape=(jax.S...]
    dot_general x16 -> x0, matrix products: 24.3 us -> none  [the longest x1 3.95 us: mixer_grads(): jnp.einsum('cshp,csn->chpn', grads_f * from_start[..., None], out_maps, p...]
    select_n x16 -> x0, other arithmetic: 17.2 us -> none  [turn(): return jax.tree.map(lambda a, b: jnp.where(reached, a, b), new, before)]
    psum x1 -> x0, blocking collectives: 10.4 us -> none  [mixer_grads(): lax.psum((in_map_part.reshape(local_rows, state_size), out_map_part.resha...]
    unnamed x23 -> x30, local copies, waits for them, and re-layouts: 4.32 us -> 12.5 us
  transfers between devices with their start and end apart: 3 -> 0, of which waited for: 2 -> 0; matrix products, arithmetic and copies ran while one was open for 15% -> 0% of each run, Pallas kernels for 0% -> 0%
where the time goes in v1:
time: 46.9 us; the launch traced here: 46.1 us
  Pallas kernels  32.9 us (70%)
  local copies, waits for them, and re-layouts  12.5 us (27%)
  between operations  0.66 us (1%)
    pallas_call x1, Pallas kernels, local(): pl.pallas_call(functools.partial(kernel, n, ntp, heads), out_shape=(jax.S...  32.9 us
    unnamed x30, local copies, waits for them, and re-layouts  12.5 us

profile of v1, /device:TPU:25, one launch (start us, length us, event | category | flops | bytes accessed | tf_op | source)
XLA Modules:
  0.0 46.1 jit_solution(7358793205904564417)
XLA Ops:
  0.6 0.0 copy-start.8
  0.6 0.7 %copy-done.8 = f32[128,16]{0,1:T(8,128)S(1)} copy-done((f32[128,16]{0,1:T(8,128)S(1)}, f32[128,16]{0,1:T(8,128)}, u32[]{:S(2)}) %copy-start.8) | copy-done | bytes 8216
  1.3 0.0 copy-start.9
  1.3 0.1 copy.17.bm_ref
  1.4 0.6 %copy-done.9 = f32[128,16]{0,1:T(8,128)S(1)} copy-done((f32[128,16]{0,1:T(8,128)S(1)}, f32[128,16]{0,1:T(8,128)}, u32[]{:S(2)}) %copy-start.9) | copy-done | bytes 8216
  2.0 0.0 copy-start.7
  2.0 0.1 copy.18.cm_ref
  2.1 0.6 %copy-done.7 = f32[128,32]{0,1:T(8,128)S(1)} copy-done((f32[128,32]{0,1:T(8,128)S(1)}, f32[128,32]{0,1:T(8,128)}, u32[]{:S(2)}) %copy-start.7) | copy-done | bytes 16408
  2.8 0.1 copy.19.dl_ref
  2.8 0.7 %copy-done.5 = bf16[128,1,128]{2,0,1:T(8,128)(2,1)S(1)} copy-done((bf16[128,1,128]{2,0,1:T(8,128)(2,1)S(1)}, bf16[128,1,128]{2,0,1:T(8,128)(2,1)}, u32[]{:S(2)}) %copy-start.5) | copy-done | bytes 32792
  3.5 0.0 copy-done.6
  3.5 1.0 %copy-done = bf16[128,2048]{1,0:T(8,128)(2,1)S(1)} copy-done((bf16[128,2048]{1,0:T(8,128)(2,1)S(1)}, bf16[128,2048]{1,0:T(8,128)(2,1)}, u32[]{:S(2)}) %copy-start) | copy-done | bytes 524312
  4.6 1.0 %copy-done.1 = bf16[128,2048]{1,0:T(8,128)(2,1)S(1)} copy-done((bf16[128,2048]{1,0:T(8,128)(2,1)S(1)}, bf16[128,2048]{1,0:T(8,128)(2,1)}, u32[]{:S(2)}) %copy-start.1) | copy-done | bytes 524312
  5.6 0.9 %copy-done.2 = bf16[128,8,128]{2,1,0:T(8,128)(2,1)S(1)} copy-done((bf16[128,8,128]{2,1,0:T(8,128)(2,1)S(1)}, bf16[128,8,128]{2,1,0:T(8,128)(2,1)}, u32[]{:S(2)}) %copy-start.2) | copy-done | bytes 262168
  6.6 0.9 %copy-done.3 = bf16[128,8,128]{2,1,0:T(8,128)(2,1)S(1)} copy-done((bf16[128,8,128]{2,1,0:T(8,128)(2,1)S(1)}, bf16[128,8,128]{2,1,0:T(8,128)(2,1)}, u32[]{:S(2)}) %copy-start.3) | copy-done | bytes 262168
  7.5 0.9 %copy-done.4 = bf16[128,8,128]{2,1,0:T(8,128)(2,1)S(1)} copy-done((bf16[128,8,128]{2,1,0:T(8,128)(2,1)S(1)}, bf16[128,8,128]{2,1,0:T(8,128)(2,1)}, u32[]{:S(2)}) %copy-start.4) | copy-done | bytes 262168
  8.5 32.9 %layer_grads.1 = (bf16[1024,128]{1,0:T(8,128)(2,1)S(1)}, bf16[128,128]{1,0:T(8,128)(2,1)S(1)}, bf16[128,128]{1,0:T(8,128)(2,1)S(1)}, bf16[128,2048]{1,0:T(8,128)...) custom-call(bf16[1024,128]{1,0:T(8,128)(2,1)S(1)} %bitcast.9, ...), custom_call_target="tpu_custom_call" | custom-call | tf_op jit(solution)/shard_map/layer_grads/pallas_call | solution.py:415
  41.3 0.7 %copy.20 = f32[128,16]{0,1:T(8,128)} copy(f32[128,16]{1,0:T(8,128)S(1)} %get-tuple-element.25) | data formatting | bytes 16384
  42.0 0.7 %copy.21 = f32[128,16]{0,1:T(8,128)} copy(f32[128,16]{1,0:T(8,128)S(1)} %get-tuple-element.26) | data formatting | bytes 16384
  42.7 0.7 %copy.22 = f32[128,32]{0,1:T(8,128)} copy(f32[128,32]{1,0:T(8,128)S(1)} %get-tuple-element.27) | data formatting | bytes 32768
  43.4 0.7 %copy.27 = bf16[128,8,128]{2,1,0:T(8,128)(2,1)} copy(bf16[128,8,128]{2,1,0:T(8,128)(2,1)S(1)} %bitcast.8) | data formatting | bytes 524288
  44.1 0.6 %copy.28 = bf16[128,1,128]{2,0,1:T(8,128)(2,1)} copy(bf16[128,1,128]{2,0,1:T(8,128)(2,1)S(1)} %bitcast.15) | data formatting | bytes 65536
  44.7 0.6 %copy.29 = bf16[128,1,128]{2,0,1:T(8,128)(2,1)} copy(bf16[128,1,128]{2,0,1:T(8,128)(2,1)S(1)} %bitcast.14) | data formatting | bytes 65536
  45.3 0.8 %copy.30 = bf16[128,2048]{1,0:T(8,128)(2,1)} copy(bf16[128,2048]{1,0:T(8,128)(2,1)S(1)} %get-tuple-element.38) | data formatting | bytes 1048576
  (7 shorter events, 0.0 us)
Async XLA Ops:
  0.6 0.7 %copy-start.8 = (f32[128,16]{0,1:T(8,128)S(1)}, f32[128,16]{0,1:T(8,128)}, u32[]{:S(2)}) copy-start(f32[128,16]{0,1:T(8,128)} %param.17) | copy-start | bytes 24580
  1.3 0.7 %copy-start.9 = (f32[128,16]{0,1:T(8,128)S(1)}, f32[128,16]{0,1:T(8,128)}, u32[]{:S(2)}) copy-start(f32[128,16]{0,1:T(8,128)} %param.18) | copy-start | bytes 24580
  2.0 0.7 %copy-start.7 = (f32[128,32]{0,1:T(8,128)S(1)}, f32[128,32]{0,1:T(8,128)}, u32[]{:S(2)}) copy-start(f32[128,32]{0,1:T(8,128)} %param.19) | copy-start | bytes 49156
  2.7 0.8 %copy-start.5 = (bf16[128,1,128]{2,0,1:T(8,128)(2,1)S(1)}, bf16[128,1,128]{2,0,1:T(8,128)(2,1)}, u32[]{:S(2)}) copy-start(bf16[128,1,128]{2,0,1:T(8,128)(2,1)} %param.11) | copy-start | bytes 98308
  2.7 0.8 %copy-start.6 = (bf16[128,1,128]{2,0,1:T(8,128)(2,1)S(1)}, bf16[128,1,128]{2,0,1:T(8,128)(2,1)}, u32[]{:S(2)}) copy-start(bf16[128,1,128]{2,0,1:T(8,128)(2,1)} %param.12) | copy-start | bytes 98308
  3.5 1.0 %copy-start = (bf16[128,2048]{1,0:T(8,128)(2,1)S(1)}, bf16[128,2048]{1,0:T(8,128)(2,1)}, u32[]{:S(2)}) copy-start(bf16[128,2048]{1,0:T(8,128)(2,1)} %x_ref.1) | copy-start | bytes 1572868
  4.6 1.0 %copy-start.1 = (bf16[128,2048]{1,0:T(8,128)(2,1)S(1)}, bf16[128,2048]{1,0:T(8,128)(2,1)}, u32[]{:S(2)}) copy-start(bf16[128,2048]{1,0:T(8,128)(2,1)} %g_ref.1) | copy-start | bytes 1572868
  5.6 0.9 %copy-start.2 = (bf16[128,8,128]{2,1,0:T(8,128)(2,1)S(1)}, bf16[128,8,128]{2,1,0:T(8,128)(2,1)}, u32[]{:S(2)}) copy-start(bf16[128,8,128]{2,1,0:T(8,128)(2,1)} %param.10) | copy-start | bytes 786436
  6.6 0.9 %copy-start.3 = (bf16[128,8,128]{2,1,0:T(8,128)(2,1)S(1)}, bf16[128,8,128]{2,1,0:T(8,128)(2,1)}, u32[]{:S(2)}) copy-start(bf16[128,8,128]{2,1,0:T(8,128)(2,1)} %param.13) | copy-start | bytes 786436
  7.5 0.9 %copy-start.4 = (bf16[128,8,128]{2,1,0:T(8,128)(2,1)S(1)}, bf16[128,8,128]{2,1,0:T(8,128)(2,1)}, u32[]{:S(2)}) copy-start(bf16[128,8,128]{2,1,0:T(8,128)(2,1)} %param.14) | copy-start | bytes 786436

commit v2 on v1

--- a/solution.py
+++ b/solution.py
@@ -48,9 +48,31 @@
     n,
     ntp,
     heads,
+    q_hbm,
+    k_hbm,
+    v_hbm,
+    o_hbm,
+    go_hbm,
+    x_hbm,
+    g_hbm,
+    bm_hbm,
+    cm_hbm,
+    dl_hbm,
+    gq_hbm,
+    gk_hbm,
+    gv_hbm,
+    gx_hbm,
+    gb_hbm,
+    gc_hbm,
+    gd_hbm,
+    gq_ref,
+    gk_ref,
+    gv_ref,
+    gx_ref,
+    gb_ref,
+    gc_ref,
+    gd_ref,
     q_ref,
-    k_ref,
-    v_ref,
     o_ref,
     go_ref,
     x_ref,
@@ -58,19 +80,14 @@
     bm_ref,
     cm_ref,
     dl_ref,
-    gq_ref,
-    gk_ref,
-    gv_ref,
-    gx_ref,
-    gb_ref,
-    gc_ref,
-    gd_ref,
     kv,
     st,
     st_out,
     tot,
     grad_out,
     grad_in,
+    grad_mid,
+    grad_own,
     tp_buf,
     gs,
     xs,
@@ -82,26 +99,70 @@
     stat_max,
     stat_sum,
     gq_t,
+    load_s,
+    store_s,
     kv_s,
     kv_r,
+    kv_f,
     st_s,
     st_r,
+    st_f,
     tt_s,
     tt_r,
     gr_s,
     gr_r,
+    gm_r,
     tp_s,
     tp_r,
 ):
     me = lax.axis_index("ctx")
     me_tp = lax.axis_index("tp")
     tokens, channels = x_ref.shape
-    groups = dl_ref.shape[1]
-    state = bm_ref.shape[1]
+    groups = dl_ref.shape[0]
+    state = bm_ref.shape[0]
+    column = lax.rem(me, 2)
+    level = me // 2
+    levels = n // 2
+    partner = me + 1 - 2 * column
     rows, width = q_ref.shape
     chunk = 256
     score_scale = 1.0 / math.sqrt(width)
 
+    loads = [
+        pltpu.make_async_copy(src, dst, load_s.at[at])
+        for at, (src, dst) in enumerate(
+            (
+                (k_hbm, kv.at[me, pl.ds(0, tokens), :]),
+                (v_hbm, kv.at[me, pl.ds(tokens, tokens), :]),
+                (dl_hbm, dl_ref),
+                (bm_hbm, bm_ref),
+                (cm_hbm, cm_ref),
+                (g_hbm, g_ref),
+                (x_hbm, x_ref),
+                (q_hbm, q_ref),
+                (go_hbm, go_ref),
+                (o_hbm, o_ref),
+            )
+        )
+    ]
+    for load in loads:
+        load.start()
+
+    stores = [
+        pltpu.make_async_copy(src, dst, store_s.at[at])
+        for at, (src, dst) in enumerate(
+            (
+                (gq_ref, gq_hbm),
+                (gk_ref, gk_hbm),
+                (gv_ref, gv_hbm),
+                (gx_ref, gx_hbm),
+                (gb_ref, gb_hbm),
+                (gc_ref, gc_hbm),
+                (gd_ref, gd_hbm),
+            )
+        )
+    ]
+
     barrier = pltpu.get_barrier_semaphore()
 
     def greet_ctx(d, c):
@@ -118,8 +179,8 @@
 
     lax.fori_loop(1, n, greet_ctx, 0)
     lax.fori_loop(1, ntp, greet_tp, 0)
-    kv[me, 0:tokens, :] = k_ref[...]
-    kv[me, tokens : 2 * tokens, :] = v_ref[...]
+    loads[0].wait()
+    loads[1].wait()
     pl.semaphore_wait(barrier, n - 1 + ntp - 1)
 
     def kv_copy(src, dst):
@@ -132,6 +193,26 @@
             device_id_type=MESH,
         )
 
+    def kv_forward(src):
+        return pltpu.make_async_remote_copy(
+            src_ref=kv.at[src],
+            dst_ref=kv.at[src],
+            send_sem=kv_f.at[src],
+            recv_sem=kv_r.at[src],
+            device_id={"ctx": partner},
+            device_id_type=MESH,
+        )
+
+    def state_forward(src):
+        return pltpu.make_async_remote_copy(
+            src_ref=st.at[src],
+            dst_ref=st.at[src],
+            send_sem=st_f.at[src],
+            recv_sem=st_r.at[src],
+            device_id={"ctx": partner},
+            device_id_type=MESH,
+        )
+
     def state_copy(src, dst, which):
         return pltpu.make_async_remote_copy(
             src_ref=st_out.at[which],
@@ -162,6 +243,16 @@
             device_id_type=MESH,
         )
 
+    def grad_pair(dst):
+        return pltpu.make_async_remote_copy(
+            src_ref=grad_out.at[dst],
+            dst_ref=grad_mid.at[dst // 2],
+            send_sem=gr_s.at[dst],
+            recv_sem=gm_r.at[dst // 2],
+            device_id={"ctx": partner},
+            device_id_type=MESH,
+        )
+
     def tp_copy(src, dst):
         return pltpu.make_async_remote_copy(
             src_ref=tp_buf.at[src],
@@ -172,11 +263,17 @@
             device_id_type=MESH,
         )
 
-    def send_kv(dst, c):
-        kv_copy(me, dst).start()
-        return c
-
-    lax.fori_loop(me + 1, n, send_kv, 0)
+    @pl.when(column == 0)
+    def _():
+        kv_copy(me, partner).start()
+
+    def send_kv(d, c):
+        kv_copy(me, 2 * (levels - 1 - d) + column).start()
+        return c
+
+    lax.fori_loop(0, levels - 1 - level, send_kv, 0)
+    for load in loads[2:]:
+        load.wait()
 
     token_row = lax.broadcasted_iota(jnp.int32, (tokens, tokens), 0)
     token_col = lax.broadcasted_iota(jnp.int32, (tokens, tokens), 1)
@@ -185,7 +282,12 @@
         lax.broadcasted_iota(jnp.int32, (groups, channels), 1) // (channels // groups)
         == lax.broadcasted_iota(jnp.int32, (groups, channels), 0)
     ).astype(F32).astype(BF16)
-    cum = mm_full(lower.astype(F32), dl_ref[...])
+
+    def tall(wide):
+        pad = jnp.zeros((128 - wide.shape[0], tokens), F32)
+        return jnp.concatenate([wide, pad], axis=0).T[:, 0 : wide.shape[0]]
+
+    cum = mm_full(lower.astype(F32), tall(dl_ref[...]))
     total = cum[tokens - 1 : tokens, :]
     mid = 0.5 * total
     e_wide[...] = mm_split(jnp.exp(cum - mid), seg)
@@ -193,13 +295,11 @@
     half_wide[...] = mm_split(jnp.exp(jnp.broadcast_to(mid, (state, groups))), seg)
     gs[0:tokens, :] = (e_wide[...] * g_ref[...].astype(F32)).astype(BF16)
     xs[0:tokens, :] = (f_wide[...] * x_ref[...].astype(F32)).astype(BF16)
-    in_map = bm_ref[...]
-    out_map = cm_ref[...]
-    maps_t = jnp.concatenate(
-        [in_map, out_map, jnp.zeros((tokens, 128 - 2 * state), F32)], axis=1
-    ).T
-    in_map_t = maps_t[0:state, :]
-    out_map_t = maps_t[state : 2 * state, :]
+    in_map_t = bm_ref[...]
+    out_map_t = cm_ref[...]
+    maps = tall(jnp.concatenate([in_map_t, out_map_t], axis=0))
+    in_map = maps[:, 0:state]
+    out_map = maps[:, state : 2 * state]
     ends_pre[...] = mm_split(in_map_t, xs[0:tokens, :])
     st_out[0] = (half_wide[...] * ends_pre[...]).astype(BF16)
     st_out[1] = (half_wide[...] * mm_split(out_map_t, gs[0:tokens, :])).astype(BF16)
@@ -207,21 +307,22 @@
         jnp.concatenate([total, jnp.zeros((1, 128 - groups), F32)], axis=1), (8, 128)
     )
 
-    def send_states(d, c):
-        dst = lax.rem(me + d, n)
-        tot_copy(me, dst).start()
-
-        @pl.when(dst > me)
-        def _():
-            state_copy(me, dst, 0).start()
-
-        @pl.when(dst < me)
-        def _():
-            state_copy(me, dst, 1).start()
-
-        return c
-
-    lax.fori_loop(1, n, send_states, 0)
+    def send_tot(d, c):
+        tot_copy(me, lax.rem(me + d, n)).start()
+        return c
+
+    def send_ends(d, c):
+        state_copy(me, 2 * (levels - 1 - d) + column, 0).start()
+        return c
+
+    def send_pulls(at, c):
+        state_copy(me, 2 * at + column, 1).start()
+        return c
+
+    lax.fori_loop(1, n, send_tot, 0)
+    state_copy(me, partner, column).start()
+    lax.fori_loop(0, levels - 1 - level, send_ends, 0)
+    lax.fori_loop(0, level, send_pulls, 0)
 
     key_at = lax.broadcasted_iota(jnp.int32, (tokens, chunk), 0)
     pair_at = lax.broadcasted_iota(jnp.int32, (tokens, chunk), 1)
@@ -239,7 +340,7 @@
             scores = jnp.where(key_at <= (pair_at + first) // heads, scores, MASKED)
         return scores
 
-    own_keys = k_ref[...]
+    own_keys = kv[me, 0:tokens, :]
     for first in range(0, rows, chunk):
         part = pl.ds(first, chunk)
         scores = scores_of(own_keys, first, True)
@@ -249,9 +350,7 @@
             jnp.sum(jnp.exp2(scores - top), axis=0, keepdims=True), (8, chunk)
         )
 
-    def stats_step(d, c):
-        src = me - d
-        kv_copy(src, me).wait_recv()
+    def stats_of(src):
         keys = kv[src, 0:tokens, :]
         for first in range(0, rows, chunk):
             part = pl.ds(first, chunk)
@@ -263,9 +362,28 @@
             )
             stat_max[:, part] = jnp.broadcast_to(top, (8, chunk))
             stat_sum[:, part] = jnp.broadcast_to(summed, (8, chunk))
-        return c
-
-    lax.fori_loop(1, me + 1, stats_step, 0)
+
+    def stats_step(d, c):
+        src = 2 * (level - d) + column
+        across = 2 * (level - d + 1) + 1 - column
+        kv_copy(src, me).wait_recv()
+        kv_forward(src).start()
+        stats_of(src)
+
+        @pl.when(across < me)
+        def _():
+            kv_copy(across, me).wait_recv()
+            stats_of(across)
+
+        return c
+
+    lax.fori_loop(1, level + 1, stats_step, 0)
+
+    @pl.when(me > 0)
+    def _():
+        kv_copy(1 - column, me).wait_recv()
+        stats_of(1 - column)
+
     stat_max[...] = stat_max[...] + jnp.log(stat_sum[...]) * LOG2E
     gq_t[...] = jnp.zeros_like(gq_t)
 
@@ -285,23 +403,64 @@
             gq_t[:, part] += mm(keys_t, grad_scores)
         return key_sum, value_sum
 
-    def grads_step(src, c):
+    def grads_across(src):
         key_sum, value_sum = grads_of(kv[src, 0:tokens, :], kv[src, tokens : 2 * tokens, :], False)
         grad_out[src, 0:tokens, :] = key_sum.astype(BF16)
         grad_out[src, tokens : 2 * tokens, :] = value_sum.astype(BF16)
-        grad_copy(me, src).start()
-        return c
-
-    lax.fori_loop(0, me, grads_step, 0)
-    own_key_sum, own_value_sum = grads_of(own_keys, v_ref[...], True)
+
+    def pass_on(at):
+        dst = 2 * at + column
+        grad_pair(dst).wait_recv()
+        grad_out[dst] = (grad_own[at] + grad_mid[at].astype(F32)).astype(BF16)
+        grad_copy(me, dst).start()
+
+    def grads_step(at, c):
+        across = 2 * at + 1 - column
+        grads_across(across)
+        grad_pair(across).start()
+        src = 2 * at + column
+        key_sum, value_sum = grads_of(kv[src, 0:tokens, :], kv[src, tokens : 2 * tokens, :], False)
+        grad_own[at, 0:tokens, :] = key_sum
+        grad_own[at, tokens : 2 * tokens, :] = value_sum
+
+        @pl.when(at > 0)
+        def _():
+            pass_on(at - 1)
+
+        return c
+
+    lax.fori_loop(0, level, grads_step, 0)
+
+    @pl.when(column == 1)
+    def _():
+        grads_across(partner)
+        grad_copy(me, partner).start()
+
+    @pl.when(level > 0)
+    def _():
+        pass_on(level - 1)
+
+    def forward_states(d, c):
+        src = lax.rem(me + 2 * d, n)
+        state_copy(src, me, 0).wait_recv()
+        state_forward(src).start()
+        return c
+
+    lax.fori_loop(1, levels, forward_states, 0)
+    own_key_sum, own_value_sum = grads_of(own_keys, kv[me, tokens : 2 * tokens, :], True)
     gq_ref[...] = gq_t[...].T.astype(BF16)
+    stores[0].start()
 
     def take_states(start, src_of):
         def step(d, carry):
             summed, log_sum = carry
             src = src_of(d)
             tot_copy(src, me).wait_recv()
-            state_copy(src, me, 0).wait_recv()
+
+            @pl.when(lax.rem(src, 2) != column)
+            def _():
+                state_copy(src, me, 0).wait_recv()
+
             summed = summed + mm_split(jnp.exp(log_sum), seg) * st[src].astype(F32)
             log_sum = log_sum + jnp.broadcast_to(tot[src][0:1, 0:groups], (state, groups))
             return summed, log_sum
@@ -311,14 +470,18 @@
 
     state_in = take_states(me + 1, lambda d: me - d) * half_wide[...]
     pull_in = take_states(n - me, lambda d: me + d) * half_wide[...]
-    xs[tokens : tokens + state, :] = state_in.astype(BF16)
-    gs[tokens : tokens + state, :] = pull_in.astype(BF16)
+    for ref, arrived in ((xs, state_in), (gs, pull_in)):
+        high, low = halves(arrived)
+        ref[tokens : tokens + state, :] = high
+        ref[tokens + state : tokens + 2 * state, :] = low
     kernel_sum = jnp.where(lower, mm_nt(gs[0:tokens, :], xs[0:tokens, :]), 0.0)
-    tp_buf[me_tp, 0:state, :] = mm_full(out_map_t, kernel_sum) + mm_nt(
-        gs[tokens : tokens + state, :], xs[0:tokens, :]
-    )
-    tp_buf[me_tp, state : 2 * state, :] = mm_full(in_map_t, kernel_sum.T) + mm_nt(
-        xs[tokens : tokens + state, :], gs[0:tokens, :]
+    pulled = mm_nt(gs[tokens : tokens + 2 * state, :], xs[0:tokens, :])
+    carried = mm_nt(xs[tokens : tokens + 2 * state, :], gs[0:tokens, :])
+    tp_buf[me_tp, 0:state, :] = (
+        mm_full(out_map_t, kernel_sum) + pulled[0:state] + pulled[state : 2 * state]
+    )
+    tp_buf[me_tp, state : 2 * state, :] = (
+        mm_full(in_map_t, kernel_sum.T) + carried[0:state] + carried[state : 2 * state]
     )
 
     def send_tp(d, c):
@@ -328,20 +491,34 @@
     lax.fori_loop(1, ntp, send_tp, 0)
 
     map_dots = jnp.where(lower, mm_full(out_map, in_map_t), 0.0)
-    forward = jnp.concatenate([map_dots.astype(BF16), out_map.astype(BF16)], axis=1)
-    backward = jnp.concatenate([map_dots.T.astype(BF16), in_map.astype(BF16)], axis=1)
-    out_pre = mm(forward, xs[...])
-    in_pre = mm(backward, gs[...])
+    forward = jnp.concatenate([map_dots, out_map, out_map], axis=1)
+    backward = jnp.concatenate([map_dots.T, in_map, in_map], axis=1)
+    out_pre = mm_split(forward, xs[...])
+    in_pre = mm_split(backward, gs[...])
     gx_ref[...] = (f_wide[...] * in_pre).astype(BF16)
+    stores[3].start()
     per_token = gs[0:tokens, :].astype(F32) * out_pre - xs[0:tokens, :].astype(F32) * in_pre
     at_end = pull_in * (state_in + ends_pre[...])
     seg_token = mm_nt_split(per_token, seg)
     seg_end = mm_nt_split(at_end, seg)
-    gd_ref[...] = mm_full((token_row <= token_col).astype(F32), seg_token) + jnp.sum(
+    grad_decay = mm_full((token_row <= token_col).astype(F32), seg_token) + jnp.sum(
         seg_end, axis=0, keepdims=True
     )
-
-    def take_grads(src, carry):
+    gd_ref[...] = jnp.concatenate(
+        [grad_decay, jnp.zeros((tokens, 128 - groups), F32)], axis=1
+    ).T[0:groups, :]
+    stores[6].start()
+
+    @pl.when(column == 0)
+    def _():
+        grad_copy(partner, me).wait_recv()
+
+    @pl.when(column == 1)
+    def _():
+        grad_in[partner] = jnp.zeros((2 * tokens, width), BF16)
+
+    def take_grads(at, carry):
+        src = 2 * at + column
         grad_copy(src, me).wait_recv()
         return (
             carry[0] + grad_in[src, 0:tokens, :].astype(F32),
@@ -349,10 +526,18 @@
         )
 
     key_total, value_total = lax.fori_loop(
-        me + 1, n, take_grads, (own_key_sum, own_value_sum)
+        level + 1,
+        levels,
+        take_grads,
+        (
+            own_key_sum + grad_in[partner, 0:tokens, :].astype(F32),
+            own_value_sum + grad_in[partner, tokens : 2 * tokens, :].astype(F32),
+        ),
     )
     gk_ref[...] = key_total.astype(BF16)
     gv_ref[...] = value_total.astype(BF16)
+    stores[1].start()
+    stores[2].start()
 
     def wait_tp(d, c):
         tp_copy(lax.rem(me_tp + d, ntp), me_tp).wait_recv()
@@ -362,22 +547,31 @@
     map_grads = tp_buf[0]
     for other in range(1, ntp):
         map_grads = map_grads + tp_buf[other]
-    map_grads = jnp.concatenate([map_grads, jnp.zeros((128 - 2 * state, tokens), F32)], axis=0).T
-    gb_ref[...] = map_grads[:, 0:state]
-    gc_ref[...] = map_grads[:, state : 2 * state]
+    gb_ref[...] = map_grads[0:state, :]
+    gc_ref[...] = map_grads[state : 2 * state, :]
+    stores[4].start()
+    stores[5].start()
 
     def end_tp(d, c):
         tp_copy(me_tp, lax.rem(me_tp + d, ntp)).wait_send()
         return c
 
+    def end_tot(d, c):
+        tot_copy(me, lax.rem(me + d, n)).wait_send()
+        return c
+
     def end_states(d, c):
-        dst = lax.rem(me + d, n)
-        tot_copy(me, dst).wait_send()
-        state_copy(me, dst, 0).wait_send()
-        return c
-
-    def end_kv(dst, c):
-        kv_copy(me, dst).wait_send()
+        other = lax.rem(me + 2 * d, n)
+        state_copy(me, other, 0).wait_send()
+        state_forward(other).wait_send()
+        return c
+
+    def end_kv(at, c):
+        kv_copy(me, 2 * at + column).wait_send()
+        return c
+
+    def end_kv_forward(at, c):
+        kv_forward(2 * at + column).wait_send()
         return c
 
     def end_grads(dst, c):
@@ -385,9 +579,31 @@
         return c
 
     lax.fori_loop(1, ntp, end_tp, 0)
-    lax.fori_loop(1, n, end_states, 0)
-    lax.fori_loop(me + 1, n, end_kv, 0)
+    lax.fori_loop(1, n, end_tot, 0)
+    state_copy(me, partner, 0).wait_send()
+    lax.fori_loop(1, levels, end_states, 0)
+
+    @pl.when(column == 0)
+    def _():
+        kv_copy(me, partner).wait_send()
+
+    lax.fori_loop(level + 1, levels, end_kv, 0)
+    lax.fori_loop(0, level, end_kv_forward, 0)
     lax.fori_loop(0, me, end_grads, 0)
+    for store in stores:
+        store.wait()
+
+
+def write_out(*refs):
+    count = len(refs) // 2
+    sems = refs[-1]
+    copies = [
+        pltpu.make_async_copy(refs[at], refs[count + at], sems.at[at]) for at in range(count)
+    ]
+    for copy in copies:
+        copy.start()
+    for copy in copies:
+        copy.wait()
 
 
 def local(
@@ -410,31 +626,43 @@
     groups = decay_log.shape[1]
     rows = tokens * heads
     flat = lambda a: a.reshape(-1, width)
-    vmem = pl.BlockSpec(memory_space=pltpu.VMEM)
+    hbm = pl.BlockSpec(memory_space=pltpu.HBM)
     dma = pltpu.SemaphoreType.DMA
+    shapes = (
+        jax.ShapeDtypeStruct((rows, width), BF16),
+        jax.ShapeDtypeStruct((tokens, width), BF16),
+        jax.ShapeDtypeStruct((tokens, width), BF16),
+        jax.ShapeDtypeStruct((tokens, channels), BF16),
+        jax.ShapeDtypeStruct((state, tokens), F32),
+        jax.ShapeDtypeStruct((state, tokens), F32),
+        jax.ShapeDtypeStruct((groups, tokens), F32),
+    )
     outs = pl.pallas_call(
         functools.partial(kernel, n, ntp, heads),
-        out_shape=(
-            jax.ShapeDtypeStruct((rows, width), BF16),
-            jax.ShapeDtypeStruct((tokens, width), BF16),
-            jax.ShapeDtypeStruct((tokens, width), BF16),
-            jax.ShapeDtypeStruct((tokens, channels), BF16),
-            jax.ShapeDtypeStruct((tokens, state), F32),
-            jax.ShapeDtypeStruct((tokens, state), F32),
-            jax.ShapeDtypeStruct((tokens, groups), F32),
-        ),
-        in_specs=[vmem] * 10,
-        out_specs=(vmem,) * 7,
-        scratch_shapes=[
+        out_shape=shapes,
+        in_specs=[hbm] * 10,
+        out_specs=(hbm,) * 7,
+        scratch_shapes=[pltpu.VMEM(out.shape, out.dtype) for out in shapes]
+        + [
+            pltpu.VMEM((rows, width), BF16),
+            pltpu.VMEM((rows, width), BF16),
+            pltpu.VMEM((rows, width), BF16),
+            pltpu.VMEM((tokens, channels), BF16),
+            pltpu.VMEM((tokens, channels), BF16),
+            pltpu.VMEM((state, tokens), F32),
+            pltpu.VMEM((state, tokens), F32),
+            pltpu.VMEM((groups, tokens), F32),
             pltpu.VMEM((n, 2 * tokens, width), BF16),
             pltpu.VMEM((n, state, channels), BF16),
             pltpu.VMEM((2, state, channels), BF16),
             pltpu.VMEM((n, 8, 128), F32),
             pltpu.VMEM((n, 2 * tokens, width), BF16),
             pltpu.VMEM((n, 2 * tokens, width), BF16),
+            pltpu.VMEM((n // 2, 2 * tokens, width), BF16),
+            pltpu.VMEM((n // 2, 2 * tokens, width), F32),
             pltpu.VMEM((ntp, 2 * state, tokens), F32),
-            pltpu.VMEM((tokens + state, channels), BF16),
-            pltpu.VMEM((tokens + state, channels), BF16),
+            pltpu.VMEM((tokens + 2 * state, channels), BF16),
+            pltpu.VMEM((tokens + 2 * state, channels), BF16),
             pltpu.VMEM((state, channels), F32),
             pltpu.VMEM((tokens, channels), F32),
             pltpu.VMEM((tokens, channels), F32),
@@ -443,19 +671,24 @@
             pltpu.VMEM((8, rows), F32),
             pltpu.VMEM((8, rows), F32),
             pltpu.VMEM((width, rows), F32),
-            dma((n,)),
-            dma((n,)),
-            dma((n,)),
-            dma((n,)),
-            dma((n,)),
-            dma((n,)),
-            dma((n,)),
-            dma((n,)),
+            dma((10,)),
+            dma((7,)),
+            dma((n,)),
+            dma((n,)),
+            dma((n,)),
+            dma((n,)),
+            dma((n,)),
+            dma((n,)),
+            dma((n,)),
+            dma((n,)),
+            dma((n,)),
+            dma((n,)),
+            dma((n // 2,)),
             dma((ntp,)),
             dma((ntp,)),
         ],
         compiler_params=pltpu.CompilerParams(
-            collective_id=0, has_side_effects=True, vmem_limit_bytes=48 * 1024 * 1024
+            collective_id=0, has_side_effects=True, vmem_limit_bytes=63 * 1024 * 1024
         ),
         name="layer_grads",
     )(
@@ -466,15 +699,24 @@
         flat(grad_attention),
         mix_input,
         grad_mix,
-        input_map,
-        output_map,
-        decay_log,
-    )
+        input_map.T,
+        output_map.T,
+        decay_log.T,
+    )
+    outs = pl.pallas_call(
+        write_out,
+        out_shape=shapes,
+        in_specs=[hbm] * 7,
+        out_specs=(hbm,) * 7,
+        compiler_params=pltpu.CompilerParams(vmem_limit_bytes=63 * 1024 * 1024),
+        scratch_shapes=[dma((7,))],
+        name="write_out",
+    )(*outs)
     return (
         outs[0].reshape(queries.shape),
         outs[1].reshape(key_vectors.shape),
         outs[2].reshape(value_vectors.shape),
-    ) + tuple(outs[3:])
+        outs[3], outs[4].T, outs[5].T, outs[6].T)
 
 
 def solution(mesh):

time: 46.9 us -> 65.7 us (1.40)
  Pallas kernels: 32.9 us -> 64 us
  local copies, waits for them, and re-layouts: 12.5 us -> 0 us
    pallas_call x1 -> x2, Pallas kernels: 32.9 us -> 64 us  [the longest x1 36 us: local(): pl.pallas_call(functools.partial(kernel, n, ntp, heads), out_shape=shapes...]
    unnamed x30 -> x0, local copies, waits for them, and re-layouts: 12.5 us -> none
where the time goes in v2:
time: 65.7 us; the launch traced here: 64.6 us
  Pallas kernels  64 us (97%)
    pallas_call x1, Pallas kernels, local(): pl.pallas_call(functools.partial(kernel, n, ntp, heads), out_shape=shapes...  36 us
    pallas_call x1, Pallas kernels, local(): pl.pallas_call(write_out, out_shape=shapes, in_specs=[hbm] * 7, out_specs...  28 us

profile of v2, /device:TPU:25, one launch (start us, length us, event | category | flops | bytes accessed | tf_op | source)
XLA Modules:
  0.0 64.6 jit_solution(12451956439998722405)
XLA Ops:
  0.6 36.0 %layer_grads.1 = (bf16[1024,128]{1,0:T(8,128)(2,1)}, bf16[128,128]{1,0:T(8,128)(2,1)}, bf16[128,128]{1,0:T(8,128)(2,1)}, bf16[128,2048]{1,0:T(8,128)(2,1)}, f32[...) custom-call(bf16[1024,128]{1,0:T(8,128)(2,1)} %bitcast.14, bf16[128,128]{1,0:T(8,128)(2,1)} %bitcast.17, ...), custom_call_target="tpu_custom_call" | custom-call | tf_op jit(solution)/shard_map/layer_grads/pallas_call | solution.py:640
  36.6 28.0 %write_out.1 = (bf16[1024,128]{1,0:T(8,128)(2,1)}, bf16[128,128]{1,0:T(8,128)(2,1)}, bf16[128,128]{1,0:T(8,128)(2,1)}, bf16[128,2048]{1,0:T(8,128)(2,1)}, f32[16...) custom-call(bf16[1024,128]{1,0:T(8,128)(2,1)} %get-tuple-element.21.refs_0_, ...), custom_call_target="tpu_custom_call" | custom-call | tf_op jit(solution)/shard_map/write_out/pallas_call | solution.py:706

commit v3 on v2

--- a/solution.py
+++ b/solution.py
@@ -95,6 +95,10 @@
     e_wide,
     f_wide,
     half_wide,
+    carry_wide,
+    out_own,
+    in_own,
+    maps_own,
     dots_row,
     stat_max,
     stat_sum,
@@ -350,6 +354,13 @@
             jnp.sum(jnp.exp2(scores - top), axis=0, keepdims=True), (8, chunk)
         )
 
+    kernel_sum = jnp.where(lower, mm_nt(gs[0:tokens, :], xs[0:tokens, :]), 0.0)
+    maps_own[0:state, :] = mm_full(out_map_t, kernel_sum)
+    maps_own[state : 2 * state, :] = mm_full(in_map_t, kernel_sum.T)
+    map_dots = jnp.where(lower, mm_full(out_map, in_map_t), 0.0)
+    out_own[...] = mm_split(map_dots, xs[0:tokens, :])
+    in_own[...] = mm_split(map_dots.T, gs[0:tokens, :])
+
     def stats_of(src):
         keys = kv[src, 0:tokens, :]
         for first in range(0, rows, chunk):
@@ -414,6 +425,12 @@
         grad_out[dst] = (grad_own[at] + grad_mid[at].astype(F32)).astype(BF16)
         grad_copy(me, dst).start()
 
+    def forward_states(d, c):
+        src = lax.rem(me + 2 * d, n)
+        state_copy(src, me, 0).wait_recv()
+        state_forward(src).start()
+        return c
+
     def grads_step(at, c):
         across = 2 * at + 1 - column
         grads_across(across)
@@ -427,9 +444,10 @@
         def _():
             pass_on(at - 1)
 
-        return c
+        return forward_states(at + 1, c)
 
     lax.fori_loop(0, level, grads_step, 0)
+    lax.fori_loop(level + 1, levels, forward_states, 0)
 
     @pl.when(column == 1)
     def _():
@@ -440,48 +458,42 @@
     def _():
         pass_on(level - 1)
 
-    def forward_states(d, c):
-        src = lax.rem(me + 2 * d, n)
-        state_copy(src, me, 0).wait_recv()
-        state_forward(src).start()
-        return c
-
-    lax.fori_loop(1, levels, forward_states, 0)
     own_key_sum, own_value_sum = grads_of(own_keys, kv[me, tokens : 2 * tokens, :], True)
     gq_ref[...] = gq_t[...].T.astype(BF16)
     stores[0].start()
 
-    def take_states(start, src_of):
-        def step(d, carry):
-            summed, log_sum = carry
-            src = src_of(d)
-            tot_copy(src, me).wait_recv()
-
-            @pl.when(lax.rem(src, 2) != column)
-            def _():
-                state_copy(src, me, 0).wait_recv()
-
-            summed = summed + mm_split(jnp.exp(log_sum), seg) * st[src].astype(F32)
-            log_sum = log_sum + jnp.broadcast_to(tot[src][0:1, 0:groups], (state, groups))
-            return summed, log_sum
-
-        zero = (jnp.zeros((state, channels), F32), jnp.zeros((state, groups), F32))
-        return lax.fori_loop(1, start, step, zero)[0]
-
-    state_in = take_states(me + 1, lambda d: me - d) * half_wide[...]
-    pull_in = take_states(n - me, lambda d: me + d) * half_wide[...]
+    def wait_tot(d, c):
+        tot_copy(lax.rem(me + d, n), me).wait_recv()
+        return c
+
+    lax.fori_loop(1, n, wait_tot, 0)
+    source = lax.broadcasted_iota(jnp.int32, (n, n), 0)
+    passed = lax.broadcasted_iota(jnp.int32, (n, n), 1)
+    between = ((source < passed) & (passed < me)) | ((me < passed) & (passed < source))
+    carry_log = mm_full(between.astype(F32), tot[:, 0, :])[:, 0:groups]
+    carry_wide[...] = mm_split(jnp.exp(carry_log), seg)
+
+    def take_states(src, summed):
+        @pl.when(lax.rem(src, 2) != column)
+        def _():
+            state_copy(src, me, 0).wait_recv()
+
+        return summed + carry_wide[pl.ds(src, 1), :] * st[src].astype(F32)
+
+    nothing = jnp.zeros((state, channels), F32)
+    state_in = lax.fori_loop(0, me, take_states, nothing) * half_wide[...]
+    pull_in = lax.fori_loop(me + 1, n, take_states, nothing) * half_wide[...]
     for ref, arrived in ((xs, state_in), (gs, pull_in)):
         high, low = halves(arrived)
         ref[tokens : tokens + state, :] = high
         ref[tokens + state : tokens + 2 * state, :] = low
-    kernel_sum = jnp.where(lower, mm_nt(gs[0:tokens, :], xs[0:tokens, :]), 0.0)
     pulled = mm_nt(gs[tokens : tokens + 2 * state, :], xs[0:tokens, :])
     carried = mm_nt(xs[tokens : tokens + 2 * state, :], gs[0:tokens, :])
     tp_buf[me_tp, 0:state, :] = (
-        mm_full(out_map_t, kernel_sum) + pulled[0:state] + pulled[state : 2 * state]
+        maps_own[0:state, :] + pulled[0:state] + pulled[state : 2 * state]
     )
     tp_buf[me_tp, state : 2 * state, :] = (
-        mm_full(in_map_t, kernel_sum.T) + carried[0:state] + carried[state : 2 * state]
+        maps_own[state : 2 * state, :] + carried[0:state] + carried[state : 2 * state]
     )
 
     def send_tp(d, c):
@@ -490,11 +502,10 @@
 
     lax.fori_loop(1, ntp, send_tp, 0)
 
-    map_dots = jnp.where(lower, mm_full(out_map, in_map_t), 0.0)
-    forward = jnp.concatenate([map_dots, out_map, out_map], axis=1)
-    backward = jnp.concatenate([map_dots.T, in_map, in_map], axis=1)
-    out_pre = mm_split(forward, xs[...])
-    in_pre = mm_split(backward, gs[...])
+    from_state = jnp.concatenate([out_map, out_map], axis=1)
+    from_pull = jnp.concatenate([in_map, in_map], axis=1)
+    out_pre = out_own[...] + mm_split(from_state, xs[tokens : tokens + 2 * state, :])
+    in_pre = in_own[...] + mm_split(from_pull, gs[tokens : tokens + 2 * state, :])
     gx_ref[...] = (f_wide[...] * in_pre).astype(BF16)
     stores[3].start()
     per_token = gs[0:tokens, :].astype(F32) * out_pre - xs[0:tokens, :].astype(F32) * in_pre
@@ -595,14 +606,17 @@
 
 
 def write_out(*refs):
-    count = len(refs) // 2
+    count = len(refs) // 3
+    ins, outs, held = refs[:count], refs[count : 2 * count], refs[2 * count : 3 * count]
     sems = refs[-1]
-    copies = [
-        pltpu.make_async_copy(refs[at], refs[count + at], sems.at[at]) for at in range(count)
-    ]
-    for copy in copies:
+    arrive = [pltpu.make_async_copy(ins[at], held[at], sems.at[0, at]) for at in range(count)]
+    leave = [pltpu.make_async_copy(held[at], outs[at], sems.at[1, at]) for at in range(count)]
+    for copy in arrive:
         copy.start()
-    for copy in copies:
+    for at in range(count):
+        arrive[at].wait()
+        leave[at].start()
+    for copy in leave:
         copy.wait()
 
 
@@ -667,6 +681,10 @@
             pltpu.VMEM((tokens, channels), F32),
             pltpu.VMEM((tokens, channels), F32),
             pltpu.VMEM((state, channels), F32),
+            pltpu.VMEM((n, channels), F32),
+            pltpu.VMEM((tokens, channels), F32),
+            pltpu.VMEM((tokens, channels), F32),
+            pltpu.VMEM((2 * state, tokens), F32),
             pltpu.VMEM((8, rows), F32),
             pltpu.VMEM((8, rows), F32),
             pltpu.VMEM((8, rows), F32),
@@ -709,7 +727,7 @@
         in_specs=[hbm] * 7,
         out_specs=(hbm,) * 7,
         compiler_params=pltpu.CompilerParams(vmem_limit_bytes=63 * 1024 * 1024),
-        scratch_shapes=[dma((7,))],
+        scratch_shapes=[pltpu.VMEM(out.shape, out.dtype) for out in shapes] + [dma((2, 7))],
         name="write_out",
     )(*outs)
     return (

time: 65.7 us -> 36.2 us (0.55)
  the two profiles are of different devices: /device:TPU:25 before, /device:TPU:17 now
where the time goes in v3:
time: 36.2 us; the launch traced here: 36 us
  Pallas kernels  35.4 us (98%)
  between operations  0.64 us (2%)
    pallas_call x1, Pallas kernels, local(): pl.pallas_call(functools.partial(kernel, n, ntp, heads), out_shape=shapes...  33.3 us
    pallas_call x1, Pallas kernels, local(): pl.pallas_call(write_out, out_shape=shapes, in_specs=[hbm] * 7, out_specs...  2.09 us

profile of v3, /device:TPU:17, one launch (start us, length us, event | category | flops | bytes accessed | tf_op | source)
XLA Modules:
  0.0 36.0 jit_solution(2863004810092027218)
XLA Ops:
  0.6 33.3 %layer_grads.1 = (bf16[1024,128]{1,0:T(8,128)(2,1)}, bf16[128,128]{1,0:T(8,128)(2,1)}, bf16[128,128]{1,0:T(8,128)(2,1)}, bf16[128,2048]{1,0:T(8,128)(2,1)}, f32[...) custom-call(bf16[1024,128]{1,0:T(8,128)(2,1)} %bitcast.14, bf16[128,128]{1,0:T(8,128)(2,1)} %bitcast.17, ...), custom_call_target="tpu_custom_call" | custom-call | tf_op jit(solution)/shard_map/layer_grads/pallas_call | solution.py:654
  34.0 2.1 %write_out.1 = (bf16[1024,128]{1,0:T(8,128)(2,1)}, bf16[128,128]{1,0:T(8,128)(2,1)}, bf16[128,128]{1,0:T(8,128)(2,1)}, bf16[128,2048]{1,0:T(8,128)(2,1)}, f32[16...) custom-call(bf16[1024,128]{1,0:T(8,128)(2,1)} %get-tuple-element.21.refs_0_, ...), custom_call_target="tpu_custom_call" | custom-call | tf_op jit(solution)/shard_map/write_out/pallas_call | solution.py:724

commit v4 on v3

--- a/solution.py
+++ b/solution.py
@@ -81,8 +81,14 @@
     cm_ref,
     dl_ref,
     kv,
-    st,
     st_out,
+    pair_in,
+    level_out,
+    level_in,
+    back_out,
+    back_in,
+    own_half,
+    pair_decay,
     tot,
     grad_out,
     grad_in,
@@ -207,20 +213,30 @@
             device_id_type=MESH,
         )
 
-    def state_forward(src):
+    def pair_copy():
         return pltpu.make_async_remote_copy(
-            src_ref=st.at[src],
-            dst_ref=st.at[src],
-            send_sem=st_f.at[src],
-            recv_sem=st_r.at[src],
+            src_ref=st_out.at[1 - column],
+            dst_ref=pair_in,
+            send_sem=st_f.at[0],
+            recv_sem=st_f.at[1],
             device_id={"ctx": partner},
             device_id_type=MESH,
         )
 
-    def state_copy(src, dst, which):
+    def back_copy():
         return pltpu.make_async_remote_copy(
-            src_ref=st_out.at[which],
-            dst_ref=st.at[src],
+            src_ref=back_out,
+            dst_ref=back_in,
+            send_sem=st_f.at[2],
+            recv_sem=st_f.at[3],
+            device_id={"ctx": partner},
+            device_id_type=MESH,
+        )
+
+    def level_copy(src, dst, which):
+        return pltpu.make_async_remote_copy(
+            src_ref=level_out.at[which],
+            dst_ref=level_in.at[src // 2],
             send_sem=st_s.at[dst],
             recv_sem=st_r.at[src],
             device_id={"ctx": dst},
@@ -305,8 +321,12 @@
     in_map = maps[:, 0:state]
     out_map = maps[:, state : 2 * state]
     ends_pre[...] = mm_split(in_map_t, xs[0:tokens, :])
-    st_out[0] = (half_wide[...] * ends_pre[...]).astype(BF16)
-    st_out[1] = (half_wide[...] * mm_split(out_map_t, gs[0:tokens, :])).astype(BF16)
+    ends = half_wide[...] * ends_pre[...]
+    pulls = half_wide[...] * mm_split(out_map_t, gs[0:tokens, :])
+    half = channels // 2
+    for side in range(2):
+        st_out[side, 0] = ends[:, side * half : (side + 1) * half]
+        st_out[side, 1] = pulls[:, side * half : (side + 1) * half]
     tot[me] = jnp.broadcast_to(
         jnp.concatenate([total, jnp.zeros((1, 128 - groups), F32)], axis=1), (8, 128)
     )
@@ -315,18 +335,8 @@
         tot_copy(me, lax.rem(me + d, n)).start()
         return c
 
-    def send_ends(d, c):
-        state_copy(me, 2 * (levels - 1 - d) + column, 0).start()
-        return c
-
-    def send_pulls(at, c):
-        state_copy(me, 2 * at + column, 1).start()
-        return c
-
+    pair_copy().start()
     lax.fori_loop(1, n, send_tot, 0)
-    state_copy(me, partner, column).start()
-    lax.fori_loop(0, levels - 1 - level, send_ends, 0)
-    lax.fori_loop(0, level, send_pulls, 0)
 
     key_at = lax.broadcasted_iota(jnp.int32, (tokens, chunk), 0)
     pair_at = lax.broadcasted_iota(jnp.int32, (tokens, chunk), 1)
@@ -360,6 +370,76 @@
     map_dots = jnp.where(lower, mm_full(out_map, in_map_t), 0.0)
     out_own[...] = mm_split(map_dots, xs[0:tokens, :])
     in_own[...] = mm_split(map_dots.T, gs[0:tokens, :])
+
+    def half_seg():
+        shape = (groups, half)
+        lane = lax.broadcasted_iota(jnp.int32, shape, 1) + column * half
+        match = lane // (channels // groups) == lax.broadcasted_iota(jnp.int32, shape, 0)
+        return match.astype(F32).astype(BF16)
+
+    is_first = column == 0
+
+    def in_order(mine, theirs):
+        return jnp.where(is_first, mine, theirs), jnp.where(is_first, theirs, mine)
+
+    def decay_of(device):
+        logs = jnp.broadcast_to(tot[device][0:1, 0:groups], (state, groups))
+        return mm_split(jnp.exp(logs), half_seg())
+
+    tot_copy(partner, me).wait_recv()
+    pair_copy().wait_recv()
+    decay_0, decay_1 = in_order(decay_of(me), decay_of(partner))
+    pair_decay[0] = decay_0
+    pair_decay[1] = decay_1
+    ends_0, ends_1 = in_order(st_out[column, 0], pair_in[0])
+    pulls_0, pulls_1 = in_order(st_out[column, 1], pair_in[1])
+    level_out[0] = (decay_1 * ends_0 + ends_1).astype(BF16)
+    level_out[1] = (pulls_0 + decay_0 * pulls_1).astype(BF16)
+
+    def send_ends(d, c):
+        level_copy(me, 2 * (levels - 1 - d) + column, 0).start()
+        return c
+
+    def send_pulls(at, c):
+        level_copy(me, 2 * at + column, 1).start()
+        return c
+
+    lax.fori_loop(0, levels - 1 - level, send_ends, 0)
+    lax.fori_loop(0, level, send_pulls, 0)
+
+    def return_states():
+        def wait_tot(d, c):
+            src = lax.rem(me + d, n)
+
+            @pl.when(src != partner)
+            def _():
+                tot_copy(src, me).wait_recv()
+
+            return c
+
+        lax.fori_loop(1, n, wait_tot, 0)
+        source = lax.broadcasted_iota(jnp.int32, (levels, n), 0)
+        passed = lax.broadcasted_iota(jnp.int32, (levels, n), 1) // 2
+        between = ((source < passed) & (passed < level)) | ((level < passed) & (passed < source))
+        carry_log = mm_full(between.astype(F32), tot[:, 0, :])[:, 0:groups]
+        carry_wide[...] = mm_split(jnp.exp(carry_log), half_seg())
+
+        def take_level(at, summed):
+            level_copy(2 * at + column, me, 0).wait_recv()
+            return summed + carry_wide[pl.ds(at, 1), :] * level_in[at].astype(F32)
+
+        nothing = jnp.zeros((state, half), F32)
+        before = lax.fori_loop(0, level, take_level, nothing)
+        after = lax.fori_loop(level + 1, levels, take_level, nothing)
+        first_ends = jnp.where(is_first, st_out[column, 0], pair_in[0])
+        second_pulls = jnp.where(is_first, pair_in[1], st_out[column, 1])
+        state_1 = first_ends + pair_decay[0] * before
+        pull_0 = second_pulls + pair_decay[1] * after
+        own_half[0] = jnp.where(is_first, before, state_1)
+        own_half[1] = jnp.where(is_first, pull_0, after)
+        back_out[0] = jnp.where(is_first, state_1, before)
+        back_out[1] = jnp.where(is_first, after, pull_0)
+        back_copy().start()
 
     def stats_of(src):
         keys = kv[src, 0:tokens, :]
@@ -425,13 +505,11 @@
         grad_out[dst] = (grad_own[at] + grad_mid[at].astype(F32)).astype(BF16)
         grad_copy(me, dst).start()
 
-    def forward_states(d, c):
-        src = lax.rem(me + 2 * d, n)
-        state_copy(src, me, 0).wait_recv()
-        state_forward(src).start()
-        return c
-
     def grads_step(at, c):
+        @pl.when(at == level - 1)
+        def _():
+            return_states()
+
         across = 2 * at + 1 - column
         grads_across(across)
         grad_pair(across).start()
@@ -444,10 +522,13 @@
         def _():
             pass_on(at - 1)
 
-        return forward_states(at + 1, c)
+        return c
 
     lax.fori_loop(0, level, grads_step, 0)
-    lax.fori_loop(level + 1, levels, forward_states, 0)
+
+    @pl.when(level == 0)
+    def _():
+        return_states()
 
     @pl.when(column == 1)
     def _():
@@ -462,27 +543,14 @@
     gq_ref[...] = gq_t[...].T.astype(BF16)
     stores[0].start()
 
-    def wait_tot(d, c):
-        tot_copy(lax.rem(me + d, n), me).wait_recv()
-        return c
-
-    lax.fori_loop(1, n, wait_tot, 0)
-    source = lax.broadcasted_iota(jnp.int32, (n, n), 0)
-    passed = lax.broadcasted_iota(jnp.int32, (n, n), 1)
-    between = ((source < passed) & (passed < me)) | ((me < passed) & (passed < source))
-    carry_log = mm_full(between.astype(F32), tot[:, 0, :])[:, 0:groups]
-    carry_wide[...] = mm_split(jnp.exp(carry_log), seg)
-
-    def take_states(src, summed):
-        @pl.when(lax.rem(src, 2) != column)
-        def _():
-            state_copy(src, me, 0).wait_recv()
-
-        return summed + carry_wide[pl.ds(src, 1), :] * st[src].astype(F32)
-
-    nothing = jnp.zeros((state, channels), F32)
-    state_in = lax.fori_loop(0, me, take_states, nothing) * half_wide[...]
-    pull_in = lax.fori_loop(me + 1, n, take_states, nothing) * half_wide[...]
+    back_copy().wait_recv()
+
+    def whole(which):
+        sides = in_order(own_half[which], back_in[which])
+        return jnp.concatenate(sides, axis=1) * half_wide[...]
+
+    state_in = whole(0)
+    pull_in = whole(1)
     for ref, arrived in ((xs, state_in), (gs, pull_in)):
         high, low = halves(arrived)
         ref[tokens : tokens + state, :] = high
@@ -572,9 +640,7 @@
         return c
 
     def end_states(d, c):
-        other = lax.rem(me + 2 * d, n)
-        state_copy(me, other, 0).wait_send()
-        state_forward(other).wait_send()
+        level_copy(me, lax.rem(me + 2 * d, n), 0).wait_send()
         return c
 
     def end_kv(at, c):
@@ -591,7 +657,8 @@
 
     lax.fori_loop(1, ntp, end_tp, 0)
     lax.fori_loop(1, n, end_tot, 0)
-    state_copy(me, partner, 0).wait_send()
+    pair_copy().wait_send()
+    back_copy().wait_send()
     lax.fori_loop(1, levels, end_states, 0)
 
     @pl.when(column == 0)
@@ -667,8 +734,14 @@
             pltpu.VMEM((state, tokens), F32),
             pltpu.VMEM((groups, tokens), F32),
             pltpu.VMEM((n, 2 * tokens, width), BF16),
-            pltpu.VMEM((n, state, channels), BF16),
-            pltpu.VMEM((2, state, channels), BF16),
+            pltpu.VMEM((2, 2, state, channels // 2), F32),
+            pltpu.VMEM((2, state, channels // 2), F32),
+            pltpu.VMEM((2, state, channels // 2), BF16),
+            pltpu.VMEM((n // 2, state, channels // 2), BF16),
+            pltpu.VMEM((2, state, channels // 2), F32),
+            pltpu.VMEM((2, state, channels // 2), F32),
+            pltpu.VMEM((2, state, channels // 2), F32),
+            pltpu.VMEM((2, state, channels // 2), F32),
             pltpu.VMEM((n, 8, 128), F32),
             pltpu.VMEM((n, 2 * tokens, width), BF16),
             pltpu.VMEM((n, 2 * tokens, width), BF16),
@@ -681,7 +754,7 @@
             pltpu.VMEM((tokens, channels), F32),
             pltpu.VMEM((tokens, channels), F32),
             pltpu.VMEM((state, channels), F32),
-            pltpu.VMEM((n, channels), F32),
+            pltpu.VMEM((n // 2, channels // 2), F32),
             pltpu.VMEM((tokens, channels), F32),
             pltpu.VMEM((tokens, channels), F32),
             pltpu.VMEM((2 * state, tokens), F32),

time: 36.2 us -> 35.2 us (0.972)
  the two profiles are of different devices: /device:TPU:17 before, /device:TPU:25 now
where the time goes in v4:
time: 35.2 us; the launch traced here: 35 us
  Pallas kernels  34.4 us (98%)
  between operations  0.64 us (2%)
    pallas_call x1, Pallas kernels, local(): pl.pallas_call(functools.partial(kernel, n, ntp, heads), out_shape=shapes...  32.3 us
    pallas_call x1, Pallas kernels, local(): pl.pallas_call(write_out, out_shape=shapes, in_specs=[hbm] * 7, out_specs...  2.09 us

profile of v4, /device:TPU:25, one launch (start us, length us, event | category | flops | bytes accessed | tf_op | source)
XLA Modules:
  0.0 35.0 jit_solution(10024544391807728529)
XLA Ops:
  0.6 32.3 %layer_grads.1 = (bf16[1024,128]{1,0:T(8,128)(2,1)}, bf16[128,128]{1,0:T(8,128)(2,1)}, bf16[128,128]{1,0:T(8,128)(2,1)}, bf16[128,2048]{1,0:T(8,128)(2,1)}, f32[...) custom-call(bf16[1024,128]{1,0:T(8,128)(2,1)} %bitcast.14, bf16[128,128]{1,0:T(8,128)(2,1)} %bitcast.17, ...), custom_call_target="tpu_custom_call" | custom-call | tf_op jit(solution)/shard_map/layer_grads/pallas_call | solution.py:721
  32.9 2.1 %write_out.1 = (bf16[1024,128]{1,0:T(8,128)(2,1)}, bf16[128,128]{1,0:T(8,128)(2,1)}, bf16[128,128]{1,0:T(8,128)(2,1)}, bf16[128,2048]{1,0:T(8,128)(2,1)}, f32[16...) custom-call(bf16[1024,128]{1,0:T(8,128)(2,1)} %get-tuple-element.21.refs_0_, ...), custom_call_target="tpu_custom_call" | custom-call | tf_op jit(solution)/shard_map/write_out/pallas_call | solution.py:797

commit v5 on v4

--- a/solution.py
+++ b/solution.py
@@ -457,8 +457,6 @@
     def stats_step(d, c):
         src = 2 * (level - d) + column
         across = 2 * (level - d + 1) + 1 - column
-        kv_copy(src, me).wait_recv()
-        kv_forward(src).start()
         stats_of(src)
 
         @pl.when(across < me)
@@ -468,6 +466,13 @@
 
         return c
 
+    def forward_kv(d, c):
+        src = 2 * (level - d) + column
+        kv_copy(src, me).wait_recv()
+        kv_forward(src).start()
+        return c
+
+    lax.fori_loop(1, level + 1, forward_kv, 0)
     lax.fori_loop(1, level + 1, stats_step, 0)
 
     @pl.when(me > 0)

time: 35.2 us -> 34.2 us (0.972)
  Pallas kernels: 34.4 us -> 33.4 us
    pallas_call x1, Pallas kernels: 32.3 us -> 31.3 us  [local(): pl.pallas_call(functools.partial(kernel, n, ntp, heads), out_shape=shapes...]
where the time goes in v5:
time: 34.2 us; the launch traced here: 34 us
  Pallas kernels  33.4 us (98%)
  between operations  0.64 us (2%)
    pallas_call x1, Pallas kernels, local(): pl.pallas_call(functools.partial(kernel, n, ntp, heads), out_shape=shapes...  31.3 us
    pallas_call x1, Pallas kernels, local(): pl.pallas_call(write_out, out_shape=shapes, in_specs=[hbm] * 7, out_specs...  2.09 us

profile of v5, /device:TPU:25, one launch (start us, length us, event | category | flops | bytes accessed | tf_op | source)
XLA Modules:
  0.0 34.0 jit_solution(9686337917544567435)
XLA Ops:
  0.6 31.3 %layer_grads.1 = (bf16[1024,128]{1,0:T(8,128)(2,1)}, bf16[128,128]{1,0:T(8,128)(2,1)}, bf16[128,128]{1,0:T(8,128)(2,1)}, bf16[128,2048]{1,0:T(8,128)(2,1)}, f32[...) custom-call(bf16[1024,128]{1,0:T(8,128)(2,1)} %bitcast.14, bf16[128,128]{1,0:T(8,128)(2,1)} %bitcast.17, ...), custom_call_target="tpu_custom_call" | custom-call | tf_op jit(solution)/shard_map/layer_grads/pallas_call | solution.py:726
  31.9 2.1 %write_out.1 = (bf16[1024,128]{1,0:T(8,128)(2,1)}, bf16[128,128]{1,0:T(8,128)(2,1)}, bf16[128,128]{1,0:T(8,128)(2,1)}, bf16[128,2048]{1,0:T(8,128)(2,1)}, f32[16...) custom-call(bf16[1024,128]{1,0:T(8,128)(2,1)} %get-tuple-element.21.refs_0_, ...), custom_call_target="tpu_custom_call" | custom-call | tf_op jit(solution)/shard_map/write_out/pallas_call | solution.py:802
